TPU v7x, 512 devices: a whole 4x8x8 slice. The times are simulated.
512 devices in a mesh: filt: 16 (over x, z_hi, core), rows: 32 (over y, z_lo).
Axes of the slice: x: 4, y: 8, z: 8 (z_hi: 2, z_lo: 4; z = z_hi * 4 + z_lo), core: 2. Of those that a mesh axis runs over, the one named last changes fastest.
Arguments:
- images: bfloat16 [32, 1024, 512], P('rows', 'filt'), may hold values from -6 to 6
- filters: bfloat16 [1024, 9, 1024], P('filt'), may hold values from -0.0625 to 0.0625
- cotangent: bfloat16 [32, 1024, 512], P('rows', 'filt'), may hold values from -6 to 6
Outputs:
- output: bfloat16 [32, 1024, 512], P('rows', 'filt')
- input_grad: bfloat16 [32, 512, 1024], P('rows', 'filt')
- filter_grad: float32 [1024, 9, 1024], P('filt')
All inputs are finite; a program needn't handle non-finite values.
Results may differ from a plain program's by a relative error of at most 0.001.
Values may be sent and summed in bfloat16 or wider, within the bound.
A program may use at most 64 MiB of HBM per device.

v0:
```python
import jax
import jax.numpy as jnp
from jax import lax
from jax.sharding import PartitionSpec as P


def extended(block, sides, width):
    for axis, dim in sides:
        count = lax.axis_size(axis)
        forward = [(i, i + 1) for i in range(count - 1)]
        backward = [(target, source) for source, target in forward]
        low = lax.ppermute(
            lax.slice_in_dim(block, block.shape[dim] - width, None, axis=dim), axis, forward
        )
        high = lax.ppermute(lax.slice_in_dim(block, 0, width, axis=dim), axis, backward)
        block = jnp.concatenate([low, block, high], axis=dim)
    return block


def pad_columns(block):
    return jnp.pad(block, ((0, 0), (0, 0), (1, 1)))


def on_device(images, filters, cotangent):
    row_count = images.shape[0]
    width = images.shape[2]
    in_total = filters.shape[2]
    groups = lax.axis_size("filt")
    framed_rows = extended(images, (("rows", 0),), 1)
    framed = pad_columns(lax.all_gather(framed_rows, "filt", axis=1, tiled=True))
    taps = []
    block_out = None
    for a in range(3):
        for b in range(3):
            window = framed[a : a + row_count, :, b : b + width]
            tap_weight = filters[:, 3 * a + b, :]
            term = jnp.einsum("oc,rcw->row", tap_weight, window, preferred_element_type=jnp.float32)
            block_out = term if block_out is None else block_out + term
            taps.append(
                jnp.einsum("row,rcw->oc", cotangent, window, preferred_element_type=jnp.float32)
            )
    out_acc = block_out
    block_terms = jnp.stack(taps, axis=1)
    grad_acc = block_terms
    out_acc, grad_acc = (out_acc, grad_acc)
    output = out_acc.astype(jnp.bfloat16)
    height = row_count * lax.axis_size("rows")
    summed = lax.psum(grad_acc, "rows")
    filter_grad = summed / jnp.sqrt(jnp.float32(height * width))
    grad_framed = pad_columns(extended(cotangent, (("rows", 0),), 1))
    total = jnp.zeros((lax.axis_size("filt") * (in_total // groups), row_count, width), jnp.float32)
    for a in range(3):
        for b in range(3):
            grad_window = grad_framed[2 - a : 2 - a + row_count, :, 2 - b : 2 - b + width]
            tap_weight = filters[:, 3 * a + b, :]
            total = total + jnp.einsum(
                "row,oc->crw", grad_window, tap_weight, preferred_element_type=jnp.float32
            )
    by_channel = lax.psum_scatter(total, "filt", scatter_dimension=0, tiled=True).astype(
        jnp.bfloat16
    )
    by_column = lax.all_to_all(by_channel, "filt", split_axis=2, concat_axis=0, tiled=True)
    input_grad = jnp.transpose(by_column, (1, 2, 0))
    return (output, input_grad, filter_grad)


def solution(mesh):
    return jax.shard_map(
        on_device,
        mesh=mesh,
        in_specs=(P("rows", "filt", None), P("filt", None, None), P("rows", "filt", None)),
        out_specs=(P("rows", "filt", None), P("rows", "filt", None), P("filt", None, None)),
        check_vma=False,
    )
```

profile of v0, /device:TPU:2, one launch (start us, length us, event | category | flops | bytes accessed | tf_op | source)
XLA Modules:
  0.0 1016.1 jit_solution(9572431659547572810)
XLA Ops:
  7.2 4.4 collective-permute-start
  11.7 1.3 collective-permute-start.1
  13.9 4.5 collective-permute-done.1
  18.4 1.5 pad_maximum_fusion
  20.0 4.3 collective-permute-start.2
  24.3 1.3 collective-permute-start.3
  25.6 1.4 fusion.50
  27.0 1.3 dynamic-slice
  28.9 1.8 collective-permute-done.3
  34.3 2.4 fusion
  36.7 6.0 copy.24
  42.7 59.7 %all-gather.2.cloned.1.call-done = bf16[3,1024,512]{2,1,0:T(8,128)(2,1)} async-done(((bf16[3,64,512]{2,1,0:T(8,128)(2,1)}), bf16[3,1024,512]{2,1,0:T(8,128)(2,1)}) %all-gather.2.cloned.1.call-update) | async-done | bytes 3145744 | tf_op jit(solution)/shard_map/all_gather | solution.py:30
  102.4 2.6 fusion.11
  106.2 1.2 fusion.9
  107.4 1.2 fusion.8
  109.8 1.2 fusion.6
  111.0 1.2 fusion.5
  113.4 1.2 fusion.3
  114.7 743.7 %all-reduce.7 = bf16[1024,1,512]{2,1,0:T(2,128)(2,1)} all-reduce(f32[1024,1,512]{2,1,0:T(1,128)} %copy.24), channel_id=2, replica_groups=mesh['filt'=16,'rows'=32] {'filt'}, use_global_device_ids=true, to_apply=%region_0.1.clone | all-reduce | flops 524288 | bytes 3145728
  860.1 1.4 reduce
  861.7 16.3 %all_to_all.18 = bf16[16,2,1024]{2,1,0:T(2,128)(2,1)S(1)} all-to-all(bf16[16,2,1024]{2,1,0:T(2,128)(2,1)S(1)} %reshape.132), channel_id=1, replica_groups=mesh['filt'=16,'rows'=32] {'filt'}, dimensions={0} | all-to-all | bytes 131072 | tf_op jit(solution)/shard_map/all_to_all | solution.py:62
  879.0 1.5 fusion.32
  884.7 121.2 %all-reduce.6.cloned.1.call-done = f32[64,9,1024]{2,0,1:T(8,128)} async-done(((f32[64,9,1024]{2,0,1:T(8,128)}), f32[64,9,1024]{2,0,1:T(8,128)}) %all-reduce.6.cloned.1.call-update) | async-done | bytes 2359312 | tf_op jit(solution)/shard_map/psum | solution.py:48
  1005.8 3.4 broadcast_multiply_fusion
  (41 shorter events, 15.0 us)
Async XLA Ops:
  7.2 23.5 %copy-start.3 = (bf16[1,64,512]{2,1,0:T(8,128)(2,1)S(1)}, bf16[1,64,512]{2,1,0:T(8,128)(2,1)}, u32[]{:S(2)}) copy-start(bf16[1,64,512]{2,1,0:T(8,128)(2,1)} %param.5) | copy-start | bytes 196612
  7.2 23.6 %copy-start.1 = (bf16[64,9,1024]{2,0,1:T(8,128)(2,1)S(1)}, bf16[64,9,1024]{2,0,1:T(8,128)(2,1)}, u32[]{:S(2)}) copy-start(bf16[64,9,1024]{2,0,1:T(8,128)(2,1)} %param.4) | copy-start | bytes 3538948
  7.2 95.2 %all-gather.2.cloned.1.call-start = ((), (), s32[]{:S(2)}) async-start(), calls=%async_computation.1 | async-start | bytes 3342336 | tf_op jit(solution)/shard_map/all_gather | solution.py:30
  7.2 6.6 collective-permute-start
  11.7 6.7 collective-permute-start.1
  19.9 985.9 %all-reduce.6.cloned.1.call-start = ((), (), s32[]{:S(2)}) async-start(), calls=%async_computation.2 | async-start | bytes 4718592 | tf_op jit(solution)/shard_map/psum | solution.py:48
  20.0 8.9 collective-permute-start.2
  24.3 6.4 collective-permute-start.3
  102.4 2.6 copy-start
  879.0 1.5 copy-start.2
Sparse Core Ops, SparseCore 0:
  20.1 82.2 all-gather.1
  114.8 890.9 all-reduce.5
where the time goes:
time: 1020 us
  blocking collectives  760 us (75%)
  waiting for transfers between devices  188 us (18%)
  matrix products  25.1 us (2%)
  between operations  14.9 us (1%)
  starting transfers between devices  11.4 us (1%)
    unnamed x1, blocking collectives  744 us
    psum x1, waiting for transfers between devices, on_device(): summed = lax.psum(grad_acc, 'rows')  121 us
    all_gather x1, waiting for transfers between devices, on_device(): lax.all_gather(framed_rows, 'filt', axis=1, tiled=True)  59.7 us
  transfers between devices with their start and end apart: 6, of which 5 were waited for; matrix products, arithmetic and copies ran while one was open for 2% of the time, Pallas kernels for 0%

commit v1 on v0

v1 whole, which is shorter than its diff:
```python
import functools

import jax
import jax.numpy as jnp
from jax import lax
from jax.experimental import pallas as pl
from jax.experimental.pallas import tpu as pltpu
from jax.sharding import PartitionSpec as P

X, ZH, CORES = 4, 2, 2
Y, ZL = 8, 4
TAPS = 3
SCALE_ROWS = 16
TOP = 200.0
f32 = jnp.float32
bf16 = jnp.bfloat16


def shifted(value, by):
    if by == 0:
        return value
    width = value.shape[1]
    column = lax.broadcasted_iota(jnp.int32, value.shape, 1)
    rolled = pltpu.roll(value, by % width, 1)
    return jnp.where(column == (0 if by == 1 else width - 1), 0.0, rolled)


def scale_for(block):
    largest = jnp.max(jnp.abs(block), axis=(0, 1), keepdims=True)
    return (TOP / jnp.maximum(largest, 1e-30)).astype(bf16).astype(f32)


def encode(value, scale):
    t = value * scale
    t2 = t * t
    t4 = t2 * t2
    t8 = t4 * t4
    t16 = t8 * t8
    return jnp.where(t < 0.0, -t16, t16).astype(bf16)


def decode(code, inverse):
    c = code.astype(f32)
    a = jnp.abs(c)
    root = lax.rsqrt(lax.rsqrt(lax.rsqrt(lax.rsqrt(jnp.maximum(a, 1e-37)))))
    root = jnp.where(a < 1e-37, 0.0, root) * inverse
    return jnp.where(c < 0.0, -root, root)


def pack(value, scale):
    lanes = value.shape[1] // 2
    flat = jnp.concatenate([value[:, :lanes], value[:, lanes:]], axis=0)
    return encode(flat, scale), jnp.broadcast_to(scale, (SCALE_ROWS, lanes)).astype(bf16)


def unpack(code):
    rows = code.shape[0] - SCALE_ROWS
    inverse = 1.0 / code[rows : rows + 1, :].astype(f32)
    flat = decode(code[:rows, :], inverse)
    return jnp.concatenate([flat[: rows // 2], flat[rows // 2 :]], axis=1)


def kernel(
    img_ref, filt_ref, cot_ref, out_ref, ig_ref, fg_ref,
    F, F2, G, G2, cots, S, dF, codes, got, FIN, O, OR, IGB, IGR, IGX, IGS, IGZ,
    f_sem, a_send, a_recv, b_send, b_recv, p_send, p_recv, c_send, c_recv, h_send, h_recv,
    rs_send, rs_recv, o_send, o_recv, ig_send, ig_recv, fz_send, fz_recv, fy_send, fy_recv,
):
    f, r = lax.axis_index("filt"), lax.axis_index("rows")
    x, zh, core = f // (ZH * CORES), (f // CORES) % ZH, f % CORES
    y, q = r // ZL, r % ZL
    chans, width = img_ref.shape
    part = chans // ZL
    stack = TAPS * chans

    def dev(f_to, r_to):
        return {"filt": f_to, "rows": r_to}

    def x_peer(d):
        return dev(((x + d) % X) * (ZH * CORES) + zh * CORES + core, r)

    def zl_peer(d):
        return dev(f, y * ZL + (q + d) % ZL)

    def y_peer(d):
        return dev(f, ((y + d) % Y) * ZL + q)

    partner = f + CORES - 2 * CORES * zh
    sibling = f + 1 - 2 * core
    zh_dev, core_dev = dev(partner, r), dev(sibling, r)

    sends = []

    def send(src, dst, s_sem, r_sem, to):
        copy = pltpu.make_async_remote_copy(
            src_ref=src, dst_ref=dst, send_sem=s_sem, recv_sem=r_sem,
            device_id=to, device_id_type=pl.DeviceIdType.MESH,
        )
        copy.start()
        return copy

    def arrived(dst, r_sem):
        pltpu.make_async_remote_copy(
            src_ref=dst, dst_ref=dst, send_sem=r_sem, recv_sem=r_sem,
            device_id=core_dev, device_id_type=pl.DeviceIdType.MESH,
        ).wait_recv()

    load_f = pltpu.make_async_copy(filt_ref, F, f_sem)
    load_f.start()

    barrier = pltpu.get_barrier_semaphore()

    def greet(to):
        pl.semaphore_signal(barrier, inc=1, device_id=to, device_id_type=pl.DeviceIdType.MESH)

    fixed = [x_peer(d) for d in range(1, X)] + [zl_peer(d) for d in range(1, ZL)]
    fixed += [y_peer(d) for d in range(1, Y)] + [zh_dev, core_dev]
    for to in fixed:
        greet(to)

    @pl.when((y > 0) & (q == 0))
    def _():
        for k in range(1, ZL):
            greet(dev(f, (y - 1) * ZL + k))

    @pl.when((y > 0) & (q > 0) & (q < ZL - 1))
    def _():
        greet(dev(f, (y - 1) * ZL + ZL - 1))

    @pl.when((y < Y - 1) & (q == ZL - 1))
    def _():
        for k in range(ZL - 1):
            greet(dev(f, (y + 1) * ZL + k))

    @pl.when((y < Y - 1) & (q > 0) & (q < ZL - 1))
    def _():
        greet(dev(f, (y + 1) * ZL))

    def g_block(k):
        return G.at[pl.ds(pl.multiple_of(k * chans, chans), chans), :]

    def g2_rows(k, to=q):
        at = 8 * (k // 8) + (to + 4 * (k % 2) + (k % 8) // 2) % 8
        return pl.ds(pl.multiple_of(at * part, part), part)

    def g2_block(k):
        return G2.at[g2_rows(k), :]

    def g2_piece(k, row, to=q):
        return G2.at[g2_rows(k, to), pl.ds(pl.multiple_of(row * width, width), width)]

    g_block(f)[...] = img_ref[...]
    g2_piece(f, q)[...] = img_ref[pl.ds(pl.multiple_of(q * part, part), part), :]
    cots[q + 1] = cot_ref[...]

    below = jnp.where(q == 0, ZL - 1, jnp.where(q == ZL - 1, 0, 1))
    above = jnp.where(q == ZL - 1, ZL - 1, jnp.where(q == 0, 0, 1))
    others = jnp.where(y > 0, below, 0) + jnp.where(y < Y - 1, above, 0)
    pl.semaphore_wait(barrier, len(fixed) + others)

    for d in range(1, ZL):
        to = (q + d) % ZL
        sends.append(send(
            img_ref.at[pl.ds(pl.multiple_of(to * part, part), part), :], g2_piece(f, q, to),
            p_send.at[d], p_recv.at[d], zl_peer(d),
        ))

    def gather_first(block, s_sem, r_sem):
        mine = block(f)
        sends.append(send(mine, mine, s_sem.at[0], r_sem.at[0], zh_dev))
        for d in range(1, X):
            sends.append(send(mine, mine, s_sem.at[d], r_sem.at[d], x_peer(d)))
        sends.append(send(mine, mine, s_sem.at[4], r_sem.at[4], core_dev))

    def gather_second(block, s_sem, r_sem):
        other = block(partner)
        arrived(other, r_sem.at[0])
        for d in range(1, X):
            sends.append(send(other, other, s_sem.at[4 + d], r_sem.at[4 + d], x_peer(d)))
        sends.append(send(other, other, s_sem.at[8], r_sem.at[8], core_dev))

    def gather_third(block, s_sem, r_sem):
        for d in range(1, X):
            x_from = ((x - d) % X) * (ZH * CORES) + core
            for second in range(2):
                k = x_from + CORES * (zh if second == 0 else 1 - zh)
                theirs = block(k)
                arrived(theirs, r_sem.at[d + 4 * second])
                at = 9 + 2 * (d - 1) + second
                sends.append(send(theirs, theirs, s_sem.at[at], r_sem.at[at], core_dev))

    def gather_last(block, s_sem, r_sem):
        base = 1 - core
        arrived(block(sibling), r_sem.at[4])
        arrived(block(partner + 1 - 2 * core), r_sem.at[8])
        for d in range(1, X):
            x_from = ((x - d) % X) * (ZH * CORES) + base
            for second in range(2):
                k = x_from + CORES * (zh if second == 0 else 1 - zh)
                arrived(block(k), r_sem.at[9 + 2 * (d - 1) + second])

    for d in range(1, ZL):
        sends.append(send(cot_ref, cots.at[q + 1], c_send.at[d], c_recv.at[d], zl_peer(d)))

    up = (q == ZL - 1) & (y < Y - 1)
    down = (q == 0) & (y > 0)

    def halo_copies(side):
        edge, slot = (y + 1, 0) if side == 0 else (y - 1, ZL + 1)
        return [
            pltpu.make_async_remote_copy(
                src_ref=cot_ref, dst_ref=cots.at[slot], send_sem=h_send.at[side, k],
                recv_sem=h_recv.at[side], device_id=dev(f, edge * ZL + k),
                device_id_type=pl.DeviceIdType.MESH,
            )
            for k in range(ZL)
        ]

    @pl.when(up)
    def _():
        for copy in halo_copies(0):
            copy.start()

    @pl.when(down)
    def _():
        for copy in halo_copies(1):
            copy.start()

    gather_first(g_block, a_send, a_recv)

    for d in range(1, ZL):
        arrived(g2_piece(f, (q - d) % ZL), p_recv.at[d])
    gather_first(g2_block, b_send, b_recv)

    load_f.wait()
    for k in range(TAPS * TAPS):
        F2[chans * k : chans * (k + 1), :] = F[:, k, :]

    def build(j):
        value = cots[j].astype(f32)
        for b in range(TAPS):
            S[b * chans : (b + 1) * chans, j * width : (j + 1) * width] = shifted(value, b - 1).astype(bf16)

    for d in range(1, ZL):
        arrived(cots.at[(q - d) % ZL + 1], c_recv.at[d])

    @pl.when(y == 0)
    def _():
        cots[0] = jnp.zeros_like(cot_ref)

    @pl.when(y == Y - 1)
    def _():
        cots[ZL + 1] = jnp.zeros_like(cot_ref)

    @pl.when(y > 0)
    def _():
        arrived(cots.at[0], h_recv.at[0])

    @pl.when(y < Y - 1)
    def _():
        arrived(cots.at[ZL + 1], h_recv.at[1])

    for j in range(ZL + 2):
        build(j)

    gather_second(g2_block, b_send, b_recv)
    gather_second(g_block, a_send, a_recv)

    groups = X * ZH * CORES
    cols = width // groups
    half = width // 2
    for p in range(2):
        total = None
        for a in range(TAPS):
            at = pl.multiple_of((q + 2 - a) * width + p * half, half)
            term = lax.dot_general(
                S[:, pl.ds(at, half)], F2[a * stack : (a + 1) * stack, :],
                (((0,), (0,)), ((), ())), preferred_element_type=f32,
            )
            total = term if total is None else total + term
        for k in range(groups // 2):
            g = p * (groups // 2) + k
            IGB[g % CORES, g // (ZH * CORES), (g // CORES) % ZH] = total[cols * k : cols * (k + 1)]
    sends.append(send(IGB.at[1 - core], IGR, ig_send.at[0], ig_recv.at[0], core_dev))

    gather_third(g2_block, b_send, b_recv)
    gather_third(g_block, a_send, a_recv)

    gather_last(g2_block, b_send, b_recv)
    for a in range(TAPS):
        at = (2 - a) * width
        dF[a * stack : (a + 1) * stack, :] = lax.dot_general(
            S[:, at : at + ZL * width], G2[...], (((1,), (1,)), ((), ())), preferred_element_type=f32
        )
    rows = TAPS * stack // Y
    scale = scale_for(dF[...])
    for k in range(Y):
        code, tail = pack(dF[rows * k : rows * (k + 1), :], scale)
        codes[k, : 2 * rows, :] = code
        codes[k, 2 * rows :, :] = tail
    for d in range(1, Y):
        sends.append(send(codes.at[(y + d) % Y], got.at[d], rs_send.at[d], rs_recv.at[d], y_peer(d)))

    arrived(IGR, ig_recv.at[0])
    for k in range(X):
        IGB[core, k] = IGB[core, k] + IGR[k]
    for d in range(1, X):
        sends.append(send(IGB.at[core, (x + d) % X], IGX.at[d], ig_send.at[d], ig_recv.at[d], x_peer(d)))

    gather_last(g_block, a_send, a_recv)
    for a in (0, 2, 1):
        total = None
        taps = jnp.dot(F2[a * stack : (a + 1) * stack, :], G[...], preferred_element_type=f32)
        for b in range(TAPS):
            term = shifted(taps[b * chans : (b + 1) * chans], 1 - b)
            total = term if total is None else total + term
        O[a] = total

    def out_copy(a):
        return pltpu.make_async_remote_copy(
            src_ref=O.at[a], dst_ref=OR.at[a // 2], send_sem=o_send.at[a // 2], recv_sem=o_recv.at[a // 2],
            device_id=dev(f, r + 1 - a), device_id_type=pl.DeviceIdType.MESH,
        )

    @pl.when(r < Y * ZL - 1)
    def _():
        out_copy(0).start()

    @pl.when(r > 0)
    def _():
        out_copy(2).start()

    piece = dF[pl.ds(pl.multiple_of(y * rows, rows), rows), :]
    for d in range(1, Y):
        arrived(got.at[d], rs_recv.at[d])
        piece = piece + unpack(got[d])
    piece = piece / jnp.sqrt(f32(Y * ZL * width))
    code, tail = pack(piece, scale_for(piece))
    FIN[y, q, : 2 * rows, :] = code
    FIN[y, q, 2 * rows :, :] = tail
    for d in range(1, ZL):
        sends.append(send(FIN.at[y, q], FIN.at[y, q], fz_send.at[d], fz_recv.at[d], zl_peer(d)))

    IGS[...] = IGB[core, x]
    for d in range(1, X):
        arrived(IGX.at[d], ig_recv.at[d])
        IGS[...] = IGS[...] + IGX[d]
    sends.append(send(IGS.at[1 - zh], IGZ, ig_send.at[X], ig_recv.at[X], zh_dev))

    for d in range(1, ZL):
        arrived(FIN.at[y, (q - d) % ZL], fz_recv.at[d])

    lane_group = lax.broadcasted_iota(jnp.int32, (rows, 128), 1) // 16

    def result(at):
        quarters = [unpack(FIN[at, k]) for k in range(ZL)]
        for t in range(8):
            half_at, j = t // 4, t % 4
            mine = (lane_group + (8 - j)) % ZL
            tile = quarters[0][:, 128 * half_at : 128 * (half_at + 1)]
            for k in range(1, ZL):
                tile = jnp.where(mine == k, quarters[k][:, 128 * half_at : 128 * (half_at + 1)], tile)
            if j:
                tile = pltpu.roll(tile, 128 - 16 * j, 1)
            fg_ref[pl.ds(pl.multiple_of(at * rows, 8), rows), 128 * t : 128 * (t + 1)] = tile

    def ring(step, way):
        at = (y - (step - 1)) % Y if way == 0 else (y + (step - 1)) % Y
        if step < Y // 2:
            ref = FIN.at[at]
        else:
            ref = FIN.at[at, pl.ds(way * (ZL // 2), ZL // 2)]
        return send(ref, ref, fy_send.at[way, step], fy_recv.at[way, step], y_peer(1 if way == 0 else -1))

    def ring_arrived(step, way):
        at = (y - step) % Y if way == 0 else (y + step) % Y
        if step < Y // 2:
            ref = FIN.at[at]
        else:
            ref = FIN.at[at, pl.ds(way * (ZL // 2), ZL // 2)]
        arrived(ref, fy_recv.at[way, step])

    for step in range(1, Y // 2 + 1):
        for way in range(2):
            if step > 1:
                ring_arrived(step - 1, way)
            sends.append(ring(step, way))
        if step == 1:
            result(y)
            OUT = O.at[1]

            @pl.when(r > 0)
            def _():
                arrived(OR.at[0], o_recv.at[0])
                OUT[...] = OUT[...] + OR[0]

            @pl.when(r < Y * ZL - 1)
            def _():
                arrived(OR.at[1], o_recv.at[1])
                OUT[...] = OUT[...] + OR[1]

            out_ref[...] = OUT[...].astype(bf16)
            arrived(IGZ, ig_recv.at[X])
            ig_ref[...] = (IGS[zh] + IGZ[...]).astype(bf16)
        else:
            result((y - (step - 1)) % Y)
            result((y + (step - 1)) % Y)
    for way in range(2):
        ring_arrived(Y // 2, way)
    result((y + Y // 2) % Y)

    for copy in sends:
        copy.wait_send()

    @pl.when(up)
    def _():
        for copy in halo_copies(0):
            copy.wait_send()

    @pl.when(down)
    def _():
        for copy in halo_copies(1):
            copy.wait_send()

    @pl.when(r < Y * ZL - 1)
    def _():
        out_copy(0).wait_send()

    @pl.when(r > 0)
    def _():
        out_copy(2).wait_send()


def on_device(images, filters, cotangent):
    _, chans, width = images.shape
    taps, total = filters.shape[1:]
    groups = X * ZH * CORES
    cols = width // groups
    stack = taps * chans
    piece = stack // Y
    quarter = total // ZL
    dma = pltpu.SemaphoreType.DMA
    vmem = pltpu.VMEM
    any_spec = pl.BlockSpec(memory_space=pl.ANY)
    vmem_spec = pl.BlockSpec(memory_space=pltpu.VMEM)
    code = (2 * piece + SCALE_ROWS, quarter // 2)
    output, input_grad, grad = pl.pallas_call(
        kernel,
        out_shape=(
            jax.ShapeDtypeStruct((chans, width), bf16),
            jax.ShapeDtypeStruct((cols, total), bf16),
            jax.ShapeDtypeStruct((stack, total), f32),
        ),
        in_specs=[vmem_spec, any_spec, vmem_spec],
        out_specs=(vmem_spec, vmem_spec, vmem_spec),
        scratch_shapes=[
            vmem((chans, taps, total), bf16),
            vmem((stack, total), bf16),
            vmem((total, width), bf16),
            vmem((quarter, ZL * width), bf16),
            vmem((ZL + 2, chans, width), bf16),
            vmem((TAPS * chans, (ZL + 2) * width), bf16),
            vmem((stack, quarter), f32),
            vmem((Y,) + code, bf16),
            vmem((Y,) + code, bf16),
            vmem((Y, ZL) + code, bf16),
            vmem((TAPS, chans, width), f32),
            vmem((2, chans, width), f32),
            vmem((CORES, X, ZH, cols, total), f32),
            vmem((X, ZH, cols, total), f32),
            vmem((X, ZH, cols, total), f32),
            vmem((ZH, cols, total), f32),
            vmem((cols, total), f32),
            dma,
            dma((15,)), dma((15,)),
            dma((15,)), dma((15,)),
            dma((ZL,)), dma((ZL,)),
            dma((ZL,)), dma((ZL,)),
            dma((2, ZL)), dma((2,)),
            dma((Y,)), dma((Y,)),
            dma((2,)), dma((2,)),
            dma((X + 1,)), dma((X + 1,)),
            dma((ZL,)), dma((ZL,)),
            dma((2, Y)), dma((2, Y)),
        ],
        compiler_params=pltpu.CompilerParams(
            collective_id=0, has_side_effects=True, vmem_limit_bytes=48 * 1024 * 1024
        ),
    )(images[0], filters, cotangent[0])
    grad = jnp.transpose(grad.reshape(taps, chans, total), (1, 0, 2))
    return output[None], input_grad[None], grad


def solution(mesh):
    return jax.shard_map(
        on_device,
        mesh=mesh,
        in_specs=(P("rows", "filt", None), P("filt", None, None), P("rows", "filt", None)),
        out_specs=(P("rows", "filt", None), P("rows", "filt", None), P("filt", None, None)),
        check_vma=False,
    )
```

time: 1020 us -> 89.8 us (0.09)
  the two profiles are of different devices: /device:TPU:2 before, /device:TPU:8 now
where the time goes in v1:
time: 89.8 us; the launch traced here: 89.7 us
  Pallas kernels  84.3 us (94%)
  local copies, waits for them, and re-layouts  4.73 us (5%)
    pallas_call x1, Pallas kernels, on_device(): pl.pallas_call(kernel, out_shape=(jax.ShapeDtypeStruct((chans, width), bf...  84.3 us
    unnamed x8, local copies, waits for them, and re-layouts  4.73 us

profile of v1, /device:TPU:8, one launch (start us, length us, event | category | flops | bytes accessed | tf_op | source)
XLA Modules:
  0.0 89.7 jit_solution(1889158448630075327)
XLA Ops:
  0.6 0.0 copy-start.1
  0.6 0.0 copy-start
  0.7 2.1 %copy.6.filt_ref = bf16[64,9,1024]{2,1,0:T(8,128)(2,1)S(1)} copy(bf16[64,9,1024]{2,0,1:T(8,128)(2,1)} %param.4) | data formatting | bytes 2359296 | tf_op args[1]
  2.7 0.0 copy-done.1
  2.7 0.0 copy-done
  2.7 84.3 %shard_map.58 = (bf16[64,512]{1,0:T(8,128)(2,1)S(1)}, bf16[32,1024]{1,0:T(8,128)(2,1)S(1)}, f32[576,1024]{1,0:T(8,128)S(1)}) custom-call(bf16[64,512]{1,0:T(8,128)(2,1)S(1)} %bitcast.8, bf16[64,9,1024]{2,1,0:T(8,128)(2,1)S(1)} %copy.6.filt_ref, bf16[64,512]{1,0:T(8,128)(2,1)S(1)} %bitcast.9), custom_call_target="tpu_custom_call" | custom-call | tf_op jit(solution)/shard_map/pallas_call | solution.py:447
  87.0 0.6 copy.10
  87.6 0.6 copy.11
  88.3 1.4 %copy.12 = f32[64,9,1024]{2,0,1:T(8,128)} copy(f32[64,9,1024]{2,0,1:T(8,128)S(1)} %bitcast.7) | data formatting | bytes 4718592
Async XLA Ops:
  0.6 2.1 %copy-start.1 = (bf16[1,64,512]{2,1,0:T(8,128)(2,1)S(1)}, bf16[1,64,512]{2,1,0:T(8,128)(2,1)}, u32[]{:S(2)}) copy-start(bf16[1,64,512]{2,1,0:T(8,128)(2,1)} %param.5) | copy-start | bytes 196612
  0.6 2.1 %copy-start = (bf16[1,64,512]{2,1,0:T(8,128)(2,1)S(1)}, bf16[1,64,512]{2,1,0:T(8,128)(2,1)}, u32[]{:S(2)}) copy-start(bf16[1,64,512]{2,1,0:T(8,128)(2,1)} %param.3) | copy-start | bytes 196612

commit v2 on v1

--- a/solution.py
+++ b/solution.py
@@ -62,7 +62,7 @@
 
 def kernel(
     img_ref, filt_ref, cot_ref, out_ref, ig_ref, fg_ref,
-    F, F2, G, G2, cots, S, dF, codes, got, FIN, O, OR, IGB, IGR, IGX, IGS, IGZ,
+    F2, G, G2, cots, S, dF, codes, got, FIN, O, OR, IGB, IGR, IGX, IGS, IGZ,
     f_sem, a_send, a_recv, b_send, b_recv, p_send, p_recv, c_send, c_recv, h_send, h_recv,
     rs_send, rs_recv, o_send, o_recv, ig_send, ig_recv, fz_send, fz_recv, fy_send, fy_recv,
 ):
@@ -91,6 +91,9 @@
 
     sends = []
 
+    def zh_peer(d):
+        return dev(partner, y * ZL + (q + d) % ZL)
+
     def send(src, dst, s_sem, r_sem, to):
         copy = pltpu.make_async_remote_copy(
             src_ref=src, dst_ref=dst, send_sem=s_sem, recv_sem=r_sem,
@@ -105,7 +108,7 @@
             device_id=core_dev, device_id_type=pl.DeviceIdType.MESH,
         ).wait_recv()
 
-    load_f = pltpu.make_async_copy(filt_ref, F, f_sem)
+    load_f = pltpu.make_async_copy(filt_ref, F2, f_sem)
     load_f.start()
 
     barrier = pltpu.get_barrier_semaphore()
@@ -114,7 +117,7 @@
         pl.semaphore_signal(barrier, inc=1, device_id=to, device_id_type=pl.DeviceIdType.MESH)
 
     fixed = [x_peer(d) for d in range(1, X)] + [zl_peer(d) for d in range(1, ZL)]
-    fixed += [y_peer(d) for d in range(1, Y)] + [zh_dev, core_dev]
+    fixed += [y_peer(d) for d in range(1, Y)] + [core_dev] + [zh_peer(d) for d in range(ZL)]
     for to in fixed:
         greet(to)
 
@@ -158,23 +161,21 @@
     others = jnp.where(y > 0, below, 0) + jnp.where(y < Y - 1, above, 0)
     pl.semaphore_wait(barrier, len(fixed) + others)
 
-    for d in range(1, ZL):
+    for d in list(range(ZL, 2 * ZL)) + list(range(1, ZL)):
         to = (q + d) % ZL
         sends.append(send(
             img_ref.at[pl.ds(pl.multiple_of(to * part, part), part), :], g2_piece(f, q, to),
-            p_send.at[d], p_recv.at[d], zl_peer(d),
+            p_send.at[d], p_recv.at[d], zl_peer(d) if d < ZL else zh_peer(d),
         ))
 
-    def gather_first(block, s_sem, r_sem):
+    def gather_own(block, s_sem, r_sem):
         mine = block(f)
-        sends.append(send(mine, mine, s_sem.at[0], r_sem.at[0], zh_dev))
         for d in range(1, X):
             sends.append(send(mine, mine, s_sem.at[d], r_sem.at[d], x_peer(d)))
         sends.append(send(mine, mine, s_sem.at[4], r_sem.at[4], core_dev))
 
-    def gather_second(block, s_sem, r_sem):
+    def gather_other(block, s_sem, r_sem):
         other = block(partner)
-        arrived(other, r_sem.at[0])
         for d in range(1, X):
             sends.append(send(other, other, s_sem.at[4 + d], r_sem.at[4 + d], x_peer(d)))
         sends.append(send(other, other, s_sem.at[8], r_sem.at[8], core_dev))
@@ -226,31 +227,35 @@
         for copy in halo_copies(1):
             copy.start()
 
-    gather_first(g_block, a_send, a_recv)
-
-    for d in range(1, ZL):
-        arrived(g2_piece(f, (q - d) % ZL), p_recv.at[d])
-    gather_first(g2_block, b_send, b_recv)
-
-    load_f.wait()
-    for k in range(TAPS * TAPS):
-        F2[chans * k : chans * (k + 1), :] = F[:, k, :]
+    gather_own(g_block, a_send, a_recv)
+    sends.append(send(g_block(f), g_block(f), a_send.at[0], a_recv.at[0], zh_dev))
 
     def build(j):
         value = cots[j].astype(f32)
         for b in range(TAPS):
-            S[b * chans : (b + 1) * chans, j * width : (j + 1) * width] = shifted(value, b - 1).astype(bf16)
+            at = j * width if isinstance(j, int) else pl.multiple_of(j * width, width)
+            S[b * chans : (b + 1) * chans, pl.ds(at, width)] = shifted(value, b - 1).astype(bf16)
+
+    build(q + 1)
+
+    @pl.when(y == 0)
+    def _():
+        cots[0] = jnp.zeros_like(cot_ref)
+
+    @pl.when(y == Y - 1)
+    def _():
+        cots[ZL + 1] = jnp.zeros_like(cot_ref)
+
+    for d in range(1, ZL):
+        arrived(g2_piece(f, (q - d) % ZL), p_recv.at[d])
+    gather_own(g2_block, b_send, b_recv)
+    for d in range(ZL):
+        arrived(g2_piece(partner, (q - d) % ZL), p_recv.at[ZL + d])
+    gather_other(g2_block, b_send, b_recv)
 
     for d in range(1, ZL):
         arrived(cots.at[(q - d) % ZL + 1], c_recv.at[d])
-
-    @pl.when(y == 0)
-    def _():
-        cots[0] = jnp.zeros_like(cot_ref)
-
-    @pl.when(y == Y - 1)
-    def _():
-        cots[ZL + 1] = jnp.zeros_like(cot_ref)
+        build((q - d) % ZL + 1)
 
     @pl.when(y > 0)
     def _():
@@ -260,11 +265,9 @@
     def _():
         arrived(cots.at[ZL + 1], h_recv.at[1])
 
-    for j in range(ZL + 2):
-        build(j)
-
-    gather_second(g2_block, b_send, b_recv)
-    gather_second(g_block, a_send, a_recv)
+    build(0)
+    build(ZL + 1)
+    load_f.wait()
 
     groups = X * ZH * CORES
     cols = width // groups
@@ -283,8 +286,9 @@
             IGB[g % CORES, g // (ZH * CORES), (g // CORES) % ZH] = total[cols * k : cols * (k + 1)]
     sends.append(send(IGB.at[1 - core], IGR, ig_send.at[0], ig_recv.at[0], core_dev))
 
+    arrived(g_block(partner), a_recv.at[0])
+    gather_other(g_block, a_send, a_recv)
     gather_third(g2_block, b_send, b_recv)
-    gather_third(g_block, a_send, a_recv)
 
     gather_last(g2_block, b_send, b_recv)
     for a in range(TAPS):
@@ -301,6 +305,8 @@
     for d in range(1, Y):
         sends.append(send(codes.at[(y + d) % Y], got.at[d], rs_send.at[d], rs_recv.at[d], y_peer(d)))
 
+    gather_third(g_block, a_send, a_recv)
+
     arrived(IGR, ig_recv.at[0])
     for k in range(X):
         IGB[core, k] = IGB[core, k] + IGR[k]
@@ -338,6 +344,26 @@
     code, tail = pack(piece, scale_for(piece))
     FIN[y, q, : 2 * rows, :] = code
     FIN[y, q, 2 * rows :, :] = tail
+    def quarter(c):
+        return (q + c) % ZL
+
+    def crosses(step, way, c):
+        return step < Y // 2 or c % 2 == way
+
+    def ring(step, way, c):
+        at = (y - (step - 1)) % Y if way == 0 else (y + (step - 1)) % Y
+        ref = FIN.at[at, quarter(c)]
+        to = y_peer(1 if way == 0 else -1)
+        sends.append(send(ref, ref, fy_send.at[way, step, c], fy_recv.at[way, step, c], to))
+
+    def ring_arrived(step, way, c):
+        at = (y - step) % Y if way == 0 else (y + step) % Y
+        arrived(FIN.at[at, quarter(c)], fy_recv.at[way, step, c])
+
+    early = list(sends)
+    sends.clear()
+    for way in range(2):
+        ring(1, way, 0)
     for d in range(1, ZL):
         sends.append(send(FIN.at[y, q], FIN.at[y, q], fz_send.at[d], fz_recv.at[d], zl_peer(d)))
 
@@ -347,8 +373,10 @@
         IGS[...] = IGS[...] + IGX[d]
     sends.append(send(IGS.at[1 - zh], IGZ, ig_send.at[X], ig_recv.at[X], zh_dev))
 
-    for d in range(1, ZL):
-        arrived(FIN.at[y, (q - d) % ZL], fz_recv.at[d])
+    for c in range(1, ZL):
+        arrived(FIN.at[y, quarter(c)], fz_recv.at[ZL - c])
+        for way in range(2):
+            ring(1, way, c)
 
     lane_group = lax.broadcasted_iota(jnp.int32, (rows, 128), 1) // 16
 
@@ -364,28 +392,16 @@
                 tile = pltpu.roll(tile, 128 - 16 * j, 1)
             fg_ref[pl.ds(pl.multiple_of(at * rows, 8), rows), 128 * t : 128 * (t + 1)] = tile
 
-    def ring(step, way):
-        at = (y - (step - 1)) % Y if way == 0 else (y + (step - 1)) % Y
-        if step < Y // 2:
-            ref = FIN.at[at]
-        else:
-            ref = FIN.at[at, pl.ds(way * (ZL // 2), ZL // 2)]
-        return send(ref, ref, fy_send.at[way, step], fy_recv.at[way, step], y_peer(1 if way == 0 else -1))
-
-    def ring_arrived(step, way):
-        at = (y - step) % Y if way == 0 else (y + step) % Y
-        if step < Y // 2:
-            ref = FIN.at[at]
-        else:
-            ref = FIN.at[at, pl.ds(way * (ZL // 2), ZL // 2)]
-        arrived(ref, fy_recv.at[way, step])
-
     for step in range(1, Y // 2 + 1):
-        for way in range(2):
-            if step > 1:
-                ring_arrived(step - 1, way)
-            sends.append(ring(step, way))
+        if step > 1:
+            for c in range(ZL):
+                for way in range(2):
+                    ring_arrived(step - 1, way, c)
+                    if crosses(step, way, c):
+                        ring(step, way, c)
         if step == 1:
+            for copy in early:
+                copy.wait_send()
             result(y)
             OUT = O.at[1]
 
@@ -405,8 +421,8 @@
         else:
             result((y - (step - 1)) % Y)
             result((y + (step - 1)) % Y)
-    for way in range(2):
-        ring_arrived(Y // 2, way)
+    for c in range(ZL):
+        ring_arrived(Y // 2, c % 2, c)
     result((y + Y // 2) % Y)
 
     for copy in sends:
@@ -436,8 +452,8 @@
     taps, total = filters.shape[1:]
     groups = X * ZH * CORES
     cols = width // groups
-    stack = taps * chans
-    piece = stack // Y
+    stack = TAPS * chans
+    piece = taps * chans // Y
     quarter = total // ZL
     dma = pltpu.SemaphoreType.DMA
     vmem = pltpu.VMEM
@@ -449,18 +465,17 @@
         out_shape=(
             jax.ShapeDtypeStruct((chans, width), bf16),
             jax.ShapeDtypeStruct((cols, total), bf16),
-            jax.ShapeDtypeStruct((stack, total), f32),
+            jax.ShapeDtypeStruct((taps * chans, total), f32),
         ),
         in_specs=[vmem_spec, any_spec, vmem_spec],
         out_specs=(vmem_spec, vmem_spec, vmem_spec),
         scratch_shapes=[
-            vmem((chans, taps, total), bf16),
-            vmem((stack, total), bf16),
+            vmem((taps * chans, total), bf16),
             vmem((total, width), bf16),
             vmem((quarter, ZL * width), bf16),
             vmem((ZL + 2, chans, width), bf16),
-            vmem((TAPS * chans, (ZL + 2) * width), bf16),
-            vmem((stack, quarter), f32),
+            vmem((stack, (ZL + 2) * width), bf16),
+            vmem((taps * chans, quarter), f32),
             vmem((Y,) + code, bf16),
             vmem((Y,) + code, bf16),
             vmem((Y, ZL) + code, bf16),
@@ -474,19 +489,19 @@
             dma,
             dma((15,)), dma((15,)),
             dma((15,)), dma((15,)),
-            dma((ZL,)), dma((ZL,)),
+            dma((2 * ZL,)), dma((2 * ZL,)),
             dma((ZL,)), dma((ZL,)),
             dma((2, ZL)), dma((2,)),
             dma((Y,)), dma((Y,)),
             dma((2,)), dma((2,)),
             dma((X + 1,)), dma((X + 1,)),
             dma((ZL,)), dma((ZL,)),
-            dma((2, Y)), dma((2, Y)),
+            dma((2, Y, ZL)), dma((2, Y, ZL)),
         ],
         compiler_params=pltpu.CompilerParams(
             collective_id=0, has_side_effects=True, vmem_limit_bytes=48 * 1024 * 1024
         ),
-    )(images[0], filters, cotangent[0])
+    )(images[0], jnp.transpose(filters, (1, 0, 2)).reshape(stack * TAPS, total), cotangent[0])
     grad = jnp.transpose(grad.reshape(taps, chans, total), (1, 0, 2))
     return output[None], input_grad[None], grad
 

time: 89.8 us -> 79.2 us (0.88)
  the two profiles are of different devices: /device:TPU:8 before, /device:TPU:4 now
where the time goes in v2:
time: 79.2 us; the launch traced here: 79 us
  Pallas kernels  72.7 us (92%)
  local copies, waits for them, and re-layouts  5.61 us (7%)
    pallas_call x1, Pallas kernels, on_device(): pl.pallas_call(kernel, out_shape=(jax.ShapeDtypeStruct((chans, width), bf...  72.7 us
    unnamed x9, local copies, waits for them, and re-layouts  5.61 us

profile of v2, /device:TPU:4, one launch (start us, length us, event | category | flops | bytes accessed | tf_op | source)
XLA Modules:
  0.0 79.0 jit_solution(12533612781199989595)
XLA Ops:
  0.6 0.0 copy-start
  0.6 1.3 %copy-done = bf16[64,9,1024]{2,0,1:T(8,128)(2,1)S(1)} copy-done((bf16[64,9,1024]{2,0,1:T(8,128)(2,1)S(1)}, bf16[64,9,1024]{2,0,1:T(8,128)(2,1)}, u32[]{:S(2)}) %copy-start) | copy-done | bytes 1179672
  1.9 0.0 copy-start.1
  1.9 0.8 %copy-done.1 = bf16[1,64,512]{2,1,0:T(8,128)(2,1)S(1)} copy-done((bf16[1,64,512]{2,1,0:T(8,128)(2,1)S(1)}, bf16[1,64,512]{2,1,0:T(8,128)(2,1)}, u32[]{:S(2)}) %copy-start.1) | copy-done | bytes 65560
  2.7 0.0 copy-start.2
  2.7 0.8 %copy-done.2 = bf16[1,64,512]{2,1,0:T(8,128)(2,1)S(1)} copy-done((bf16[1,64,512]{2,1,0:T(8,128)(2,1)S(1)}, bf16[1,64,512]{2,1,0:T(8,128)(2,1)}, u32[]{:S(2)}) %copy-start.2) | copy-done | bytes 65560
  3.6 72.7 %shard_map.58 = (bf16[64,512]{1,0:T(8,128)(2,1)S(1)}, bf16[32,1024]{1,0:T(8,128)(2,1)S(1)}, f32[576,1024]{1,0:T(8,128)S(1)}) custom-call(bf16[64,512]{1,0:T(8,128)(2,1)S(1)} %bitcast.12, bf16[576,1024]{1,0:T(8,128)(2,1)S(1)} %bitcast.11, bf16[64,512]{1,0:T(8,128)(2,1)S(1)} %bitcast.13), custom_call_target="tpu_custom_call" | custom-call | tf_op jit(solution)/shard_map/pallas_call | solution.py:463
  76.3 0.6 copy.9
  77.0 0.6 copy.10
  77.6 1.4 %copy.11 = f32[64,9,1024]{2,0,1:T(8,128)} copy(f32[64,9,1024]{2,0,1:T(8,128)S(1)} %bitcast.10) | data formatting | bytes 4718592
Async XLA Ops:
  0.6 1.3 %copy-start = (bf16[64,9,1024]{2,0,1:T(8,128)(2,1)S(1)}, bf16[64,9,1024]{2,0,1:T(8,128)(2,1)}, u32[]{:S(2)}) copy-start(bf16[64,9,1024]{2,0,1:T(8,128)(2,1)} %param.4) | copy-start | bytes 3538948
  1.9 0.8 %copy-start.1 = (bf16[1,64,512]{2,1,0:T(8,128)(2,1)S(1)}, bf16[1,64,512]{2,1,0:T(8,128)(2,1)}, u32[]{:S(2)}) copy-start(bf16[1,64,512]{2,1,0:T(8,128)(2,1)} %param.3) | copy-start | bytes 196612
  2.7 0.8 %copy-start.2 = (bf16[1,64,512]{2,1,0:T(8,128)(2,1)S(1)}, bf16[1,64,512]{2,1,0:T(8,128)(2,1)}, u32[]{:S(2)}) copy-start(bf16[1,64,512]{2,1,0:T(8,128)(2,1)} %param.5) | copy-start | bytes 196612

commit v3 on v2

--- a/solution.py
+++ b/solution.py
@@ -108,8 +108,14 @@
             device_id=core_dev, device_id_type=pl.DeviceIdType.MESH,
         ).wait_recv()
 
-    load_f = pltpu.make_async_copy(filt_ref, F2, f_sem)
-    load_f.start()
+    def g_block(k):
+        return G.at[pl.ds(pl.multiple_of(k * chans, chans), chans), :]
+
+    load_img = pltpu.make_async_copy(img_ref, g_block(f), f_sem.at[0])
+    load_cot = pltpu.make_async_copy(cot_ref, cots.at[q + 1], f_sem.at[1])
+    load_f = pltpu.make_async_copy(filt_ref, F2, f_sem.at[2])
+    for load in (load_img, load_cot, load_f):
+        load.start()
 
     barrier = pltpu.get_barrier_semaphore()
 
@@ -121,26 +127,15 @@
     for to in fixed:
         greet(to)
 
-    @pl.when((y > 0) & (q == 0))
-    def _():
-        for k in range(1, ZL):
-            greet(dev(f, (y - 1) * ZL + k))
-
-    @pl.when((y > 0) & (q > 0) & (q < ZL - 1))
-    def _():
-        greet(dev(f, (y - 1) * ZL + ZL - 1))
-
-    @pl.when((y < Y - 1) & (q == ZL - 1))
-    def _():
-        for k in range(ZL - 1):
-            greet(dev(f, (y + 1) * ZL + k))
-
-    @pl.when((y < Y - 1) & (q > 0) & (q < ZL - 1))
-    def _():
-        greet(dev(f, (y + 1) * ZL))
-
-    def g_block(k):
-        return G.at[pl.ds(pl.multiple_of(k * chans, chans), chans), :]
+    below, above = (y > 0) & (q == 0), (y < Y - 1) & (q == ZL - 1)
+
+    @pl.when(below)
+    def _():
+        greet(dev(f, r - 1))
+
+    @pl.when(above)
+    def _():
+        greet(dev(f, r + 1))
 
     def g2_rows(k, to=q):
         at = 8 * (k // 8) + (to + 4 * (k % 2) + (k % 8) // 2) % 8
@@ -152,19 +147,16 @@
     def g2_piece(k, row, to=q):
         return G2.at[g2_rows(k, to), pl.ds(pl.multiple_of(row * width, width), width)]
 
-    g_block(f)[...] = img_ref[...]
-    g2_piece(f, q)[...] = img_ref[pl.ds(pl.multiple_of(q * part, part), part), :]
-    cots[q + 1] = cot_ref[...]
-
-    below = jnp.where(q == 0, ZL - 1, jnp.where(q == ZL - 1, 0, 1))
-    above = jnp.where(q == ZL - 1, ZL - 1, jnp.where(q == 0, 0, 1))
-    others = jnp.where(y > 0, below, 0) + jnp.where(y < Y - 1, above, 0)
+    load_img.wait()
+    load_cot.wait()
+    g2_piece(f, q)[...] = G[pl.ds(pl.multiple_of(f * chans + q * part, part), part), :]
+    others = jnp.where(below, 1, 0) + jnp.where(above, 1, 0)
     pl.semaphore_wait(barrier, len(fixed) + others)
 
     for d in list(range(ZL, 2 * ZL)) + list(range(1, ZL)):
         to = (q + d) % ZL
         sends.append(send(
-            img_ref.at[pl.ds(pl.multiple_of(to * part, part), part), :], g2_piece(f, q, to),
+            G.at[pl.ds(pl.multiple_of(f * chans + to * part, part), part), :], g2_piece(f, q, to),
             p_send.at[d], p_recv.at[d], zl_peer(d) if d < ZL else zh_peer(d),
         ))
 
@@ -201,34 +193,15 @@
                 arrived(block(k), r_sem.at[9 + 2 * (d - 1) + second])
 
     for d in range(1, ZL):
-        sends.append(send(cot_ref, cots.at[q + 1], c_send.at[d], c_recv.at[d], zl_peer(d)))
-
-    up = (q == ZL - 1) & (y < Y - 1)
-    down = (q == 0) & (y > 0)
-
-    def halo_copies(side):
-        edge, slot = (y + 1, 0) if side == 0 else (y - 1, ZL + 1)
-        return [
-            pltpu.make_async_remote_copy(
-                src_ref=cot_ref, dst_ref=cots.at[slot], send_sem=h_send.at[side, k],
-                recv_sem=h_recv.at[side], device_id=dev(f, edge * ZL + k),
-                device_id_type=pl.DeviceIdType.MESH,
-            )
-            for k in range(ZL)
-        ]
-
-    @pl.when(up)
-    def _():
-        for copy in halo_copies(0):
-            copy.start()
-
-    @pl.when(down)
-    def _():
-        for copy in halo_copies(1):
-            copy.start()
-
-    gather_own(g_block, a_send, a_recv)
-    sends.append(send(g_block(f), g_block(f), a_send.at[0], a_recv.at[0], zh_dev))
+        mine = cots.at[q + 1]
+        sends.append(send(mine, mine, c_send.at[d], c_recv.at[d], zl_peer(d)))
+
+    def halo_copy(side):
+        source, slot, step = (ZL, 0, 1) if side == 0 else (1, ZL + 1, -1)
+        return pltpu.make_async_remote_copy(
+            src_ref=cots.at[source], dst_ref=cots.at[slot], send_sem=h_send.at[side],
+            recv_sem=h_recv.at[side], device_id=y_peer(step), device_id_type=pl.DeviceIdType.MESH,
+        )
 
     def build(j):
         value = cots[j].astype(f32)
@@ -249,13 +222,40 @@
     for d in range(1, ZL):
         arrived(g2_piece(f, (q - d) % ZL), p_recv.at[d])
     gather_own(g2_block, b_send, b_recv)
+    sends.append(send(g_block(f), g_block(f), a_send.at[0], a_recv.at[0], zh_dev))
     for d in range(ZL):
         arrived(g2_piece(partner, (q - d) % ZL), p_recv.at[ZL + d])
     gather_other(g2_block, b_send, b_recv)
+    gather_own(g_block, a_send, a_recv)
 
     for d in range(1, ZL):
         arrived(cots.at[(q - d) % ZL + 1], c_recv.at[d])
+
+    @pl.when(y < Y - 1)
+    def _():
+        halo_copy(0).start()
+
+    @pl.when(y > 0)
+    def _():
+        halo_copy(1).start()
+
+    for d in range(1, ZL):
         build((q - d) % ZL + 1)
+
+    gather_third(g2_block, b_send, b_recv)
+
+    gather_last(g2_block, b_send, b_recv)
+
+    def grad_term(a, first, last):
+        at = (2 - a + first) * width
+        return lax.dot_general(
+            S[:, at : at + (last - first) * width], G2[:, first * width : last * width],
+            (((1,), (1,)), ((), ())), preferred_element_type=f32,
+        )
+
+    dF[stack : 2 * stack, :] = grad_term(1, 0, ZL)
+    dF[:stack, :] = grad_term(0, 0, ZL - 1)
+    dF[2 * stack :, :] = grad_term(2, 1, ZL)
 
     @pl.when(y > 0)
     def _():
@@ -267,8 +267,19 @@
 
     build(0)
     build(ZL + 1)
+
+    dF[:stack, :] += grad_term(0, ZL - 1, ZL)
+    dF[2 * stack :, :] += grad_term(2, 0, 1)
+    rows = TAPS * stack // Y
+    scale = scale_for(dF[...])
+    for k in range(Y):
+        code, tail = pack(dF[rows * k : rows * (k + 1), :], scale)
+        codes[k, : 2 * rows, :] = code
+        codes[k, 2 * rows :, :] = tail
+    for d in range(1, Y):
+        sends.append(send(codes.at[(y + d) % Y], got.at[d], rs_send.at[d], rs_recv.at[d], y_peer(d)))
+
     load_f.wait()
-
     groups = X * ZH * CORES
     cols = width // groups
     half = width // 2
@@ -288,24 +299,6 @@
 
     arrived(g_block(partner), a_recv.at[0])
     gather_other(g_block, a_send, a_recv)
-    gather_third(g2_block, b_send, b_recv)
-
-    gather_last(g2_block, b_send, b_recv)
-    for a in range(TAPS):
-        at = (2 - a) * width
-        dF[a * stack : (a + 1) * stack, :] = lax.dot_general(
-            S[:, at : at + ZL * width], G2[...], (((1,), (1,)), ((), ())), preferred_element_type=f32
-        )
-    rows = TAPS * stack // Y
-    scale = scale_for(dF[...])
-    for k in range(Y):
-        code, tail = pack(dF[rows * k : rows * (k + 1), :], scale)
-        codes[k, : 2 * rows, :] = code
-        codes[k, 2 * rows :, :] = tail
-    for d in range(1, Y):
-        sends.append(send(codes.at[(y + d) % Y], got.at[d], rs_send.at[d], rs_recv.at[d], y_peer(d)))
-
-    gather_third(g_block, a_send, a_recv)
 
     arrived(IGR, ig_recv.at[0])
     for k in range(X):
@@ -313,28 +306,7 @@
     for d in range(1, X):
         sends.append(send(IGB.at[core, (x + d) % X], IGX.at[d], ig_send.at[d], ig_recv.at[d], x_peer(d)))
 
-    gather_last(g_block, a_send, a_recv)
-    for a in (0, 2, 1):
-        total = None
-        taps = jnp.dot(F2[a * stack : (a + 1) * stack, :], G[...], preferred_element_type=f32)
-        for b in range(TAPS):
-            term = shifted(taps[b * chans : (b + 1) * chans], 1 - b)
-            total = term if total is None else total + term
-        O[a] = total
-
-    def out_copy(a):
-        return pltpu.make_async_remote_copy(
-            src_ref=O.at[a], dst_ref=OR.at[a // 2], send_sem=o_send.at[a // 2], recv_sem=o_recv.at[a // 2],
-            device_id=dev(f, r + 1 - a), device_id_type=pl.DeviceIdType.MESH,
-        )
-
-    @pl.when(r < Y * ZL - 1)
-    def _():
-        out_copy(0).start()
-
-    @pl.when(r > 0)
-    def _():
-        out_copy(2).start()
+    gather_third(g_block, a_send, a_recv)
 
     piece = dF[pl.ds(pl.multiple_of(y * rows, rows), rows), :]
     for d in range(1, Y):
@@ -367,11 +339,28 @@
     for d in range(1, ZL):
         sends.append(send(FIN.at[y, q], FIN.at[y, q], fz_send.at[d], fz_recv.at[d], zl_peer(d)))
 
-    IGS[...] = IGB[core, x]
-    for d in range(1, X):
-        arrived(IGX.at[d], ig_recv.at[d])
-        IGS[...] = IGS[...] + IGX[d]
-    sends.append(send(IGS.at[1 - zh], IGZ, ig_send.at[X], ig_recv.at[X], zh_dev))
+    gather_last(g_block, a_send, a_recv)
+    for a in (0, 2, 1):
+        total = None
+        taps = jnp.dot(F2[a * stack : (a + 1) * stack, :], G[...], preferred_element_type=f32)
+        for b in range(TAPS):
+            term = shifted(taps[b * chans : (b + 1) * chans], 1 - b)
+            total = term if total is None else total + term
+        O[a] = total
+
+    def out_copy(a):
+        return pltpu.make_async_remote_copy(
+            src_ref=O.at[a], dst_ref=OR.at[a // 2], send_sem=o_send.at[a // 2], recv_sem=o_recv.at[a // 2],
+            device_id=dev(f, r + 1 - a), device_id_type=pl.DeviceIdType.MESH,
+        )
+
+    @pl.when(r < Y * ZL - 1)
+    def _():
+        out_copy(0).start()
+
+    @pl.when(r > 0)
+    def _():
+        out_copy(2).start()
 
     for c in range(1, ZL):
         arrived(FIN.at[y, quarter(c)], fz_recv.at[ZL - c])
@@ -403,21 +392,11 @@
             for copy in early:
                 copy.wait_send()
             result(y)
-            OUT = O.at[1]
-
-            @pl.when(r > 0)
-            def _():
-                arrived(OR.at[0], o_recv.at[0])
-                OUT[...] = OUT[...] + OR[0]
-
-            @pl.when(r < Y * ZL - 1)
-            def _():
-                arrived(OR.at[1], o_recv.at[1])
-                OUT[...] = OUT[...] + OR[1]
-
-            out_ref[...] = OUT[...].astype(bf16)
-            arrived(IGZ, ig_recv.at[X])
-            ig_ref[...] = (IGS[zh] + IGZ[...]).astype(bf16)
+            IGS[...] = IGB[core, x]
+            for d in range(1, X):
+                arrived(IGX.at[d], ig_recv.at[d])
+                IGS[...] = IGS[...] + IGX[d]
+            sends.append(send(IGS.at[1 - zh], IGZ, ig_send.at[X], ig_recv.at[X], zh_dev))
         else:
             result((y - (step - 1)) % Y)
             result((y + (step - 1)) % Y)
@@ -425,18 +404,32 @@
         ring_arrived(Y // 2, c % 2, c)
     result((y + Y // 2) % Y)
 
+    OUT = O.at[1]
+
+    @pl.when(r > 0)
+    def _():
+        arrived(OR.at[0], o_recv.at[0])
+        OUT[...] = OUT[...] + OR[0]
+
+    @pl.when(r < Y * ZL - 1)
+    def _():
+        arrived(OR.at[1], o_recv.at[1])
+        OUT[...] = OUT[...] + OR[1]
+
+    out_ref[...] = OUT[...].astype(bf16)
+    arrived(IGZ, ig_recv.at[X])
+    ig_ref[...] = (IGS[zh] + IGZ[...]).astype(bf16)
+
     for copy in sends:
         copy.wait_send()
 
-    @pl.when(up)
-    def _():
-        for copy in halo_copies(0):
-            copy.wait_send()
-
-    @pl.when(down)
-    def _():
-        for copy in halo_copies(1):
-            copy.wait_send()
+    @pl.when(y < Y - 1)
+    def _():
+        halo_copy(0).wait_send()
+
+    @pl.when(y > 0)
+    def _():
+        halo_copy(1).wait_send()
 
     @pl.when(r < Y * ZL - 1)
     def _():
@@ -457,7 +450,7 @@
     quarter = total // ZL
     dma = pltpu.SemaphoreType.DMA
     vmem = pltpu.VMEM
-    any_spec = pl.BlockSpec(memory_space=pl.ANY)
+    hbm_spec = pl.BlockSpec(memory_space=pltpu.HBM)
     vmem_spec = pl.BlockSpec(memory_space=pltpu.VMEM)
     code = (2 * piece + SCALE_ROWS, quarter // 2)
     output, input_grad, grad = pl.pallas_call(
@@ -467,7 +460,7 @@
             jax.ShapeDtypeStruct((cols, total), bf16),
             jax.ShapeDtypeStruct((taps * chans, total), f32),
         ),
-        in_specs=[vmem_spec, any_spec, vmem_spec],
+        in_specs=[hbm_spec, hbm_spec, hbm_spec],
         out_specs=(vmem_spec, vmem_spec, vmem_spec),
         scratch_shapes=[
             vmem((taps * chans, total), bf16),
@@ -486,12 +479,12 @@
             vmem((X, ZH, cols, total), f32),
             vmem((ZH, cols, total), f32),
             vmem((cols, total), f32),
-            dma,
+            dma((3,)),
             dma((15,)), dma((15,)),
             dma((15,)), dma((15,)),
             dma((2 * ZL,)), dma((2 * ZL,)),
             dma((ZL,)), dma((ZL,)),
-            dma((2, ZL)), dma((2,)),
+            dma((2,)), dma((2,)),
             dma((Y,)), dma((Y,)),
             dma((2,)), dma((2,)),
             dma((X + 1,)), dma((X + 1,)),

time: 79.2 us -> 72.4 us (0.914)
  the two profiles are of different devices: /device:TPU:4 before, /device:TPU:1 now
where the time goes in v3:
time: 72.4 us; the launch traced here: 71.9 us
  Pallas kernels  65.7 us (91%)
  local copies, waits for them, and re-layouts  5.61 us (8%)
    pallas_call x1, Pallas kernels, on_device(): pl.pallas_call(kernel, out_shape=(jax.ShapeDtypeStruct((chans, width), bf...  65.7 us
    unnamed x9, local copies, waits for them, and re-layouts  5.61 us

profile of v3, /device:TPU:1, one launch (start us, length us, event | category | flops | bytes accessed | tf_op | source)
XLA Modules:
  0.0 71.9 jit_solution(13606720959127149488)
XLA Ops:
  0.6 0.0 copy-start
  0.6 1.3 %copy-done = bf16[64,9,1024]{2,0,1:T(8,128)(2,1)S(1)} copy-done((bf16[64,9,1024]{2,0,1:T(8,128)(2,1)S(1)}, bf16[64,9,1024]{2,0,1:T(8,128)(2,1)}, u32[]{:S(2)}) %copy-start) | copy-done | bytes 1179672
  1.9 0.0 copy-start.1
  1.9 0.8 %copy-done.1 = bf16[1,64,512]{2,1,0:T(8,128)(2,1)S(1)} copy-done((bf16[1,64,512]{2,1,0:T(8,128)(2,1)S(1)}, bf16[1,64,512]{2,1,0:T(8,128)(2,1)}, u32[]{:S(2)}) %copy-start.1) | copy-done | bytes 65560
  2.7 0.0 copy-start.2
  2.7 0.8 %copy-done.2 = bf16[1,64,512]{2,1,0:T(8,128)(2,1)S(1)} copy-done((bf16[1,64,512]{2,1,0:T(8,128)(2,1)S(1)}, bf16[1,64,512]{2,1,0:T(8,128)(2,1)}, u32[]{:S(2)}) %copy-start.2) | copy-done | bytes 65560
  3.6 65.7 %shard_map.58 = (bf16[64,512]{1,0:T(8,128)(2,1)S(1)}, bf16[32,1024]{1,0:T(8,128)(2,1)S(1)}, f32[576,1024]{1,0:T(8,128)S(1)}) custom-call(bf16[64,512]{1,0:T(8,128)(2,1)S(1)} %bitcast.12, bf16[576,1024]{1,0:T(8,128)(2,1)S(1)} %bitcast.11, bf16[64,512]{1,0:T(8,128)(2,1)S(1)} %bitcast.13), custom_call_target="tpu_custom_call" | custom-call | tf_op jit(solution)/shard_map/pallas_call | solution.py:456
  69.3 0.6 copy.9
  69.9 0.6 copy.10
  70.5 1.4 %copy.11 = f32[64,9,1024]{2,0,1:T(8,128)} copy(f32[64,9,1024]{2,0,1:T(8,128)S(1)} %bitcast.10) | data formatting | bytes 4718592
Async XLA Ops:
  0.6 1.3 %copy-start = (bf16[64,9,1024]{2,0,1:T(8,128)(2,1)S(1)}, bf16[64,9,1024]{2,0,1:T(8,128)(2,1)}, u32[]{:S(2)}) copy-start(bf16[64,9,1024]{2,0,1:T(8,128)(2,1)} %param.4) | copy-start | bytes 3538948
  1.9 0.8 %copy-start.1 = (bf16[1,64,512]{2,1,0:T(8,128)(2,1)S(1)}, bf16[1,64,512]{2,1,0:T(8,128)(2,1)}, u32[]{:S(2)}) copy-start(bf16[1,64,512]{2,1,0:T(8,128)(2,1)} %param.3) | copy-start | bytes 196612
  2.7 0.8 %copy-start.2 = (bf16[1,64,512]{2,1,0:T(8,128)(2,1)S(1)}, bf16[1,64,512]{2,1,0:T(8,128)(2,1)}, u32[]{:S(2)}) copy-start(bf16[1,64,512]{2,1,0:T(8,128)(2,1)} %param.5) | copy-start | bytes 196612

commit v4 on v3

--- a/solution.py
+++ b/solution.py
@@ -61,7 +61,7 @@
 
 
 def kernel(
-    img_ref, filt_ref, cot_ref, out_ref, ig_ref, fg_ref,
+    rows_ref, filt_ref, out_ref, ig_ref, fg_ref,
     F2, G, G2, cots, S, dF, codes, got, FIN, O, OR, IGB, IGR, IGX, IGS, IGZ,
     f_sem, a_send, a_recv, b_send, b_recv, p_send, p_recv, c_send, c_recv, h_send, h_recv,
     rs_send, rs_recv, o_send, o_recv, ig_send, ig_recv, fz_send, fz_recv, fy_send, fy_recv,
@@ -69,7 +69,7 @@
     f, r = lax.axis_index("filt"), lax.axis_index("rows")
     x, zh, core = f // (ZH * CORES), (f // CORES) % ZH, f % CORES
     y, q = r // ZL, r % ZL
-    chans, width = img_ref.shape
+    _, chans, width = rows_ref.shape
     part = chans // ZL
     stack = TAPS * chans
 
@@ -111,8 +111,8 @@
     def g_block(k):
         return G.at[pl.ds(pl.multiple_of(k * chans, chans), chans), :]
 
-    load_img = pltpu.make_async_copy(img_ref, g_block(f), f_sem.at[0])
-    load_cot = pltpu.make_async_copy(cot_ref, cots.at[q + 1], f_sem.at[1])
+    load_img = pltpu.make_async_copy(rows_ref.at[0], g_block(f), f_sem.at[0])
+    load_cot = pltpu.make_async_copy(rows_ref.at[1], cots.at[q + 1], f_sem.at[1])
     load_f = pltpu.make_async_copy(filt_ref, F2, f_sem.at[2])
     for load in (load_img, load_cot, load_f):
         load.start()
@@ -196,6 +196,8 @@
         mine = cots.at[q + 1]
         sends.append(send(mine, mine, c_send.at[d], c_recv.at[d], zl_peer(d)))
 
+    gather_own(g_block, a_send, a_recv)
+
     def halo_copy(side):
         source, slot, step = (ZL, 0, 1) if side == 0 else (1, ZL + 1, -1)
         return pltpu.make_async_remote_copy(
@@ -213,11 +215,11 @@
 
     @pl.when(y == 0)
     def _():
-        cots[0] = jnp.zeros_like(cot_ref)
+        cots[0] = jnp.zeros((chans, width), bf16)
 
     @pl.when(y == Y - 1)
     def _():
-        cots[ZL + 1] = jnp.zeros_like(cot_ref)
+        cots[ZL + 1] = jnp.zeros((chans, width), bf16)
 
     for d in range(1, ZL):
         arrived(g2_piece(f, (q - d) % ZL), p_recv.at[d])
@@ -226,7 +228,6 @@
     for d in range(ZL):
         arrived(g2_piece(partner, (q - d) % ZL), p_recv.at[ZL + d])
     gather_other(g2_block, b_send, b_recv)
-    gather_own(g_block, a_send, a_recv)
 
     for d in range(1, ZL):
         arrived(cots.at[(q - d) % ZL + 1], c_recv.at[d])
@@ -245,6 +246,9 @@
     gather_third(g2_block, b_send, b_recv)
 
     gather_last(g2_block, b_send, b_recv)
+
+    arrived(g_block(partner), a_recv.at[0])
+    gather_other(g_block, a_send, a_recv)
 
     def grad_term(a, first, last):
         at = (2 - a + first) * width
@@ -297,8 +301,23 @@
             IGB[g % CORES, g // (ZH * CORES), (g // CORES) % ZH] = total[cols * k : cols * (k + 1)]
     sends.append(send(IGB.at[1 - core], IGR, ig_send.at[0], ig_recv.at[0], core_dev))
 
-    arrived(g_block(partner), a_recv.at[0])
-    gather_other(g_block, a_send, a_recv)
+
+    gather_third(g_block, a_send, a_recv)
+
+    gather_last(g_block, a_send, a_recv)
+    for a in (0, 2, 1):
+        total = None
+        taps = jnp.dot(F2[a * stack : (a + 1) * stack, :], G[...], preferred_element_type=f32)
+        for b in range(TAPS):
+            term = shifted(taps[b * chans : (b + 1) * chans], 1 - b)
+            total = term if total is None else total + term
+        O[a] = total
+
+    def out_copy(a):
+        return pltpu.make_async_remote_copy(
+            src_ref=O.at[a], dst_ref=OR.at[a // 2], send_sem=o_send.at[a // 2], recv_sem=o_recv.at[a // 2],
+            device_id=dev(f, r + 1 - a), device_id_type=pl.DeviceIdType.MESH,
+        )
 
     arrived(IGR, ig_recv.at[0])
     for k in range(X):
@@ -306,7 +325,6 @@
     for d in range(1, X):
         sends.append(send(IGB.at[core, (x + d) % X], IGX.at[d], ig_send.at[d], ig_recv.at[d], x_peer(d)))
 
-    gather_third(g_block, a_send, a_recv)
 
     piece = dF[pl.ds(pl.multiple_of(y * rows, rows), rows), :]
     for d in range(1, Y):
@@ -332,6 +350,13 @@
         at = (y - step) % Y if way == 0 else (y + step) % Y
         arrived(FIN.at[at, quarter(c)], fy_recv.at[way, step, c])
 
+    def pass_on(step, c):
+        for way in range(2):
+            if crosses(step, way, c):
+                ring_arrived(step, way, c)
+                if step < Y // 2 and crosses(step + 1, way, c):
+                    ring(step + 1, way, c)
+
     early = list(sends)
     sends.clear()
     for way in range(2):
@@ -339,33 +364,19 @@
     for d in range(1, ZL):
         sends.append(send(FIN.at[y, q], FIN.at[y, q], fz_send.at[d], fz_recv.at[d], zl_peer(d)))
 
-    gather_last(g_block, a_send, a_recv)
-    for a in (0, 2, 1):
-        total = None
-        taps = jnp.dot(F2[a * stack : (a + 1) * stack, :], G[...], preferred_element_type=f32)
-        for b in range(TAPS):
-            term = shifted(taps[b * chans : (b + 1) * chans], 1 - b)
-            total = term if total is None else total + term
-        O[a] = total
-
-    def out_copy(a):
-        return pltpu.make_async_remote_copy(
-            src_ref=O.at[a], dst_ref=OR.at[a // 2], send_sem=o_send.at[a // 2], recv_sem=o_recv.at[a // 2],
-            device_id=dev(f, r + 1 - a), device_id_type=pl.DeviceIdType.MESH,
-        )
-
-    @pl.when(r < Y * ZL - 1)
-    def _():
-        out_copy(0).start()
-
-    @pl.when(r > 0)
-    def _():
-        out_copy(2).start()
-
+    pass_on(1, 0)
     for c in range(1, ZL):
         arrived(FIN.at[y, quarter(c)], fz_recv.at[ZL - c])
         for way in range(2):
             ring(1, way, c)
+
+    @pl.when(r < Y * ZL - 1)
+    def _():
+        out_copy(0).start()
+
+    @pl.when(r > 0)
+    def _():
+        out_copy(2).start()
 
     lane_group = lax.broadcasted_iota(jnp.int32, (rows, 128), 1) // 16
 
@@ -381,27 +392,22 @@
                 tile = pltpu.roll(tile, 128 - 16 * j, 1)
             fg_ref[pl.ds(pl.multiple_of(at * rows, 8), rows), 128 * t : 128 * (t + 1)] = tile
 
+    result(y)
     for step in range(1, Y // 2 + 1):
-        if step > 1:
-            for c in range(ZL):
-                for way in range(2):
-                    ring_arrived(step - 1, way, c)
-                    if crosses(step, way, c):
-                        ring(step, way, c)
+        for c in range(1, ZL):
+            pass_on(step, c)
+        if step < Y // 2:
+            pass_on(step + 1, 0)
+            result((y - step) % Y)
+            result((y + step) % Y)
         if step == 1:
-            for copy in early:
-                copy.wait_send()
-            result(y)
             IGS[...] = IGB[core, x]
             for d in range(1, X):
                 arrived(IGX.at[d], ig_recv.at[d])
                 IGS[...] = IGS[...] + IGX[d]
             sends.append(send(IGS.at[1 - zh], IGZ, ig_send.at[X], ig_recv.at[X], zh_dev))
-        else:
-            result((y - (step - 1)) % Y)
-            result((y + (step - 1)) % Y)
-    for c in range(ZL):
-        ring_arrived(Y // 2, c % 2, c)
+            for copy in early:
+                copy.wait_send()
     result((y + Y // 2) % Y)
 
     OUT = O.at[1]
@@ -460,7 +466,7 @@
             jax.ShapeDtypeStruct((cols, total), bf16),
             jax.ShapeDtypeStruct((taps * chans, total), f32),
         ),
-        in_specs=[hbm_spec, hbm_spec, hbm_spec],
+        in_specs=[hbm_spec, hbm_spec],
         out_specs=(vmem_spec, vmem_spec, vmem_spec),
         scratch_shapes=[
             vmem((taps * chans, total), bf16),
@@ -494,7 +500,7 @@
         compiler_params=pltpu.CompilerParams(
             collective_id=0, has_side_effects=True, vmem_limit_bytes=48 * 1024 * 1024
         ),
-    )(images[0], jnp.transpose(filters, (1, 0, 2)).reshape(stack * TAPS, total), cotangent[0])
+    )(jnp.concatenate([images, cotangent]), jnp.transpose(filters, (1, 0, 2)).reshape(stack * TAPS, total))
     grad = jnp.transpose(grad.reshape(taps, chans, total), (1, 0, 2))
     return output[None], input_grad[None], grad
 

time: 72.4 us -> 69.9 us (0.965)
  local copies, waits for them, and re-layouts: 5.61 us -> 3.93 us
  Pallas kernels: 65.7 us -> 64.3 us
  other arithmetic: 0 us -> 0.89 us
    unnamed x9 -> x5, local copies, waits for them, and re-layouts: 5.61 us -> 3.93 us
    pallas_call x1, Pallas kernels: 65.7 us -> 64.3 us  [on_device(): pl.pallas_call(kernel, out_shape=(jax.ShapeDtypeStruct((chans, width), bf...]
    concatenate x0 -> x1, other arithmetic: none -> 0.89 us  [on_device(): jnp.concatenate([images, cotangent])]
where the time goes in v4:
time: 69.9 us; the launch traced here: 69.7 us
  Pallas kernels  64.3 us (92%)
  local copies, waits for them, and re-layouts  3.93 us (6%)
  other arithmetic  0.89 us (1%)
    pallas_call x1, Pallas kernels, on_device(): pl.pallas_call(kernel, out_shape=(jax.ShapeDtypeStruct((chans, width), bf...  64.3 us
    unnamed x5, local copies, waits for them, and re-layouts  3.93 us

profile of v4, /device:TPU:1, one launch (start us, length us, event | category | flops | bytes accessed | tf_op | source)
XLA Modules:
  0.0 69.7 jit_solution(5844105136572498662)
XLA Ops:
  0.6 0.9 %pad_maximum_fusion.rows_ref = bf16[2,64,512]{2,1,0:T(8,128)(2,1)S(1)} fusion(bf16[1,64,512]{2,1,0:T(8,128)(2,1)} %param.5, bf16[1,64,512]{2,1,0:T(8,128)(2,1)} %param.3), kind=kLoop, calls=%fused_computation | loop fusion | flops 65536 | bytes 262144 | tf_op jit(solution)/shard_map/concatenate | solution.py:503
  1.5 0.0 copy-start
  1.5 1.3 %copy-done = bf16[64,9,1024]{2,0,1:T(8,128)(2,1)S(1)} copy-done((bf16[64,9,1024]{2,0,1:T(8,128)(2,1)S(1)}, bf16[64,9,1024]{2,0,1:T(8,128)(2,1)}, u32[]{:S(2)}) %copy-start) | copy-done | bytes 1179672
  2.8 64.3 %shard_map.58 = (bf16[64,512]{1,0:T(8,128)(2,1)S(1)}, bf16[32,1024]{1,0:T(8,128)(2,1)S(1)}, f32[576,1024]{1,0:T(8,128)S(1)}) custom-call(bf16[2,64,512]{2,1,0:T(8,128)(2,1)S(1)} %pad_maximum_fusion.rows_ref, bf16[576,1024]{1,0:T(8,128)(2,1)S(1)} %bitcast.9), custom_call_target="tpu_custom_call" | custom-call | tf_op jit(solution)/shard_map/pallas_call | solution.py:462
  67.1 0.6 copy.9
  67.7 0.6 copy.10
  68.3 1.4 %copy.11 = f32[64,9,1024]{2,0,1:T(8,128)} copy(f32[64,9,1024]{2,0,1:T(8,128)S(1)} %bitcast.8) | data formatting | bytes 4718592
Async XLA Ops:
  1.5 1.3 %copy-start = (bf16[64,9,1024]{2,0,1:T(8,128)(2,1)S(1)}, bf16[64,9,1024]{2,0,1:T(8,128)(2,1)}, u32[]{:S(2)}) copy-start(bf16[64,9,1024]{2,0,1:T(8,128)(2,1)} %param.4) | copy-start | bytes 3538948

commit v5 on v4

--- a/solution.py
+++ b/solution.py
@@ -61,7 +61,7 @@
 
 
 def kernel(
-    rows_ref, filt_ref, out_ref, ig_ref, fg_ref,
+    img_ref, filt_ref, cot_ref, out_ref, ig_ref, fg_ref,
     F2, G, G2, cots, S, dF, codes, got, FIN, O, OR, IGB, IGR, IGX, IGS, IGZ,
     f_sem, a_send, a_recv, b_send, b_recv, p_send, p_recv, c_send, c_recv, h_send, h_recv,
     rs_send, rs_recv, o_send, o_recv, ig_send, ig_recv, fz_send, fz_recv, fy_send, fy_recv,
@@ -69,7 +69,7 @@
     f, r = lax.axis_index("filt"), lax.axis_index("rows")
     x, zh, core = f // (ZH * CORES), (f // CORES) % ZH, f % CORES
     y, q = r // ZL, r % ZL
-    _, chans, width = rows_ref.shape
+    chans, width = img_ref.shape
     part = chans // ZL
     stack = TAPS * chans
 
@@ -111,8 +111,8 @@
     def g_block(k):
         return G.at[pl.ds(pl.multiple_of(k * chans, chans), chans), :]
 
-    load_img = pltpu.make_async_copy(rows_ref.at[0], g_block(f), f_sem.at[0])
-    load_cot = pltpu.make_async_copy(rows_ref.at[1], cots.at[q + 1], f_sem.at[1])
+    load_img = pltpu.make_async_copy(img_ref, g_block(f), f_sem.at[0])
+    load_cot = pltpu.make_async_copy(cot_ref, cots.at[q + 1], f_sem.at[1])
     load_f = pltpu.make_async_copy(filt_ref, F2, f_sem.at[2])
     for load in (load_img, load_cot, load_f):
         load.start()
@@ -455,6 +455,7 @@
     piece = taps * chans // Y
     quarter = total // ZL
     dma = pltpu.SemaphoreType.DMA
+    operands = images[0], jnp.transpose(filters, (1, 0, 2)).reshape(stack * TAPS, total), cotangent[0]
     vmem = pltpu.VMEM
     hbm_spec = pl.BlockSpec(memory_space=pltpu.HBM)
     vmem_spec = pl.BlockSpec(memory_space=pltpu.VMEM)
@@ -466,7 +467,7 @@
             jax.ShapeDtypeStruct((cols, total), bf16),
             jax.ShapeDtypeStruct((taps * chans, total), f32),
         ),
-        in_specs=[hbm_spec, hbm_spec],
+        in_specs=[hbm_spec] * 3,
         out_specs=(vmem_spec, vmem_spec, vmem_spec),
         scratch_shapes=[
             vmem((taps * chans, total), bf16),
@@ -500,7 +501,7 @@
         compiler_params=pltpu.CompilerParams(
             collective_id=0, has_side_effects=True, vmem_limit_bytes=48 * 1024 * 1024
         ),
-    )(jnp.concatenate([images, cotangent]), jnp.transpose(filters, (1, 0, 2)).reshape(stack * TAPS, total))
+    )(*(pltpu.with_memory_space_constraint(a, pltpu.HBM) for a in operands))
     grad = jnp.transpose(grad.reshape(taps, chans, total), (1, 0, 2))
     return output[None], input_grad[None], grad
 

time: 69.9 us -> 67.4 us (0.964)
  local copies, waits for them, and re-layouts: 3.93 us -> 2.67 us
  other arithmetic: 0.89 us -> 0 us
    unnamed x5 -> x3, local copies, waits for them, and re-layouts: 3.93 us -> 2.67 us
    concatenate x1 -> x0, other arithmetic: 0.89 us -> none  [on_device(): jnp.concatenate([images, cotangent])]
where the time goes in v5:
time: 67.4 us; the launch traced here: 67.2 us
  Pallas kernels  63.9 us (95%)
  local copies, waits for them, and re-layouts  2.67 us (4%)
    pallas_call x1, Pallas kernels, on_device(): pl.pallas_call(kernel, out_shape=(jax.ShapeDtypeStruct((chans, width), bf...  63.9 us
    unnamed x3, local copies, waits for them, and re-layouts  2.67 us

profile of v5, /device:TPU:1, one launch (start us, length us, event | category | flops | bytes accessed | tf_op | source)
XLA Modules:
  0.0 67.2 jit_solution(11269757802980009144)
XLA Ops:
  0.6 63.9 %shard_map.58 = (bf16[64,512]{1,0:T(8,128)(2,1)S(1)}, bf16[32,1024]{1,0:T(8,128)(2,1)S(1)}, f32[576,1024]{1,0:T(8,128)S(1)}) custom-call(bf16[64,512]{1,0:T(8,128)(2,1)} %bitcast.14, bf16[576,1024]{1,0:T(8,128)(2,1)} %bitcast.13, bf16[64,512]{1,0:T(8,128)(2,1)} %bitcast.15), custom_call_target="tpu_custom_call" | custom-call | tf_op jit(solution)/shard_map/pallas_call | solution.py:463
  64.6 0.6 copy.9
  65.2 0.6 copy.10
  65.8 1.4 %copy.11 = f32[64,9,1024]{2,0,1:T(8,128)} copy(f32[64,9,1024]{2,0,1:T(8,128)S(1)} %bitcast.10) | data formatting | bytes 4718592

commit v6 on v5

--- a/solution.py
+++ b/solution.py
@@ -47,6 +47,16 @@
     return jnp.where(c < 0.0, -root, root)
 
 
+def coded(value):
+    scale = scale_for(value)
+    return encode(value, scale), jnp.broadcast_to(scale, (SCALE_ROWS, value.shape[1])).astype(bf16)
+
+
+def decoded(code):
+    rows = code.shape[0] - SCALE_ROWS
+    return decode(code[:rows, :], 1.0 / code[rows : rows + 1, :].astype(f32))
+
+
 def pack(value, scale):
     lanes = value.shape[1] // 2
     flat = jnp.concatenate([value[:, :lanes], value[:, lanes:]], axis=0)
@@ -62,9 +72,10 @@
 
 def kernel(
     img_ref, filt_ref, cot_ref, out_ref, ig_ref, fg_ref,
-    F2, G, G2, cots, S, dF, codes, got, FIN, O, OR, IGB, IGR, IGX, IGS, IGZ,
+    F2, G, G2, cots, S, dF, codes, got, FIN, O, OC, OR, IGB, IGR, IXC, IXR, IGS, IZC, IZR,
     f_sem, a_send, a_recv, b_send, b_recv, p_send, p_recv, c_send, c_recv, h_send, h_recv,
     rs_send, rs_recv, o_send, o_recv, ig_send, ig_recv, fz_send, fz_recv, fy_send, fy_recv,
+    fo_send, fo_recv, fa_send, fa_recv,
 ):
     f, r = lax.axis_index("filt"), lax.axis_index("rows")
     x, zh, core = f // (ZH * CORES), (f // CORES) % ZH, f % CORES
@@ -172,15 +183,13 @@
             sends.append(send(other, other, s_sem.at[4 + d], r_sem.at[4 + d], x_peer(d)))
         sends.append(send(other, other, s_sem.at[8], r_sem.at[8], core_dev))
 
-    def gather_third(block, s_sem, r_sem):
+    def gather_third(block, s_sem, r_sem, second):
         for d in range(1, X):
-            x_from = ((x - d) % X) * (ZH * CORES) + core
-            for second in range(2):
-                k = x_from + CORES * (zh if second == 0 else 1 - zh)
-                theirs = block(k)
-                arrived(theirs, r_sem.at[d + 4 * second])
-                at = 9 + 2 * (d - 1) + second
-                sends.append(send(theirs, theirs, s_sem.at[at], r_sem.at[at], core_dev))
+            k = ((x - d) % X) * (ZH * CORES) + core + CORES * (zh if second == 0 else 1 - zh)
+            theirs = block(k)
+            arrived(theirs, r_sem.at[d + 4 * second])
+            at = 9 + 2 * (d - 1) + second
+            sends.append(send(theirs, theirs, s_sem.at[at], r_sem.at[at], core_dev))
 
     def gather_last(block, s_sem, r_sem):
         base = 1 - core
@@ -229,6 +238,7 @@
         arrived(g2_piece(partner, (q - d) % ZL), p_recv.at[ZL + d])
     gather_other(g2_block, b_send, b_recv)
 
+    gather_third(g2_block, b_send, b_recv, 0)
     for d in range(1, ZL):
         arrived(cots.at[(q - d) % ZL + 1], c_recv.at[d])
 
@@ -243,7 +253,7 @@
     for d in range(1, ZL):
         build((q - d) % ZL + 1)
 
-    gather_third(g2_block, b_send, b_recv)
+    gather_third(g2_block, b_send, b_recv, 1)
 
     gather_last(g2_block, b_send, b_recv)
 
@@ -302,7 +312,18 @@
     sends.append(send(IGB.at[1 - core], IGR, ig_send.at[0], ig_recv.at[0], core_dev))
 
 
-    gather_third(g_block, a_send, a_recv)
+    gather_third(g_block, a_send, a_recv, 0)
+    gather_third(g_block, a_send, a_recv, 1)
+
+    arrived(IGR, ig_recv.at[0])
+    deep = ZH * cols
+    for d in range(1, X):
+        to = (x + d) % X
+        code, tail = coded((IGB[core, to] + IGR[to]).reshape(deep, -1))
+        IXC[d, :deep, :] = code
+        IXC[d, deep:, :] = tail
+        sends.append(send(IXC.at[d], IXR.at[d], ig_send.at[d], ig_recv.at[d], x_peer(d)))
+    IGS[...] = IGB[core, x] + IGR[x]
 
     gather_last(g_block, a_send, a_recv)
     for a in (0, 2, 1):
@@ -311,20 +332,18 @@
         for b in range(TAPS):
             term = shifted(taps[b * chans : (b + 1) * chans], 1 - b)
             total = term if total is None else total + term
-        O[a] = total
+        if a == 1:
+            O[...] = total
+        else:
+            code, tail = coded(total)
+            OC[a // 2, :chans, :] = code
+            OC[a // 2, chans:, :] = tail
 
     def out_copy(a):
         return pltpu.make_async_remote_copy(
-            src_ref=O.at[a], dst_ref=OR.at[a // 2], send_sem=o_send.at[a // 2], recv_sem=o_recv.at[a // 2],
+            src_ref=OC.at[a // 2], dst_ref=OR.at[a // 2], send_sem=o_send.at[a // 2], recv_sem=o_recv.at[a // 2],
             device_id=dev(f, r + 1 - a), device_id_type=pl.DeviceIdType.MESH,
         )
-
-    arrived(IGR, ig_recv.at[0])
-    for k in range(X):
-        IGB[core, k] = IGB[core, k] + IGR[k]
-    for d in range(1, X):
-        sends.append(send(IGB.at[core, (x + d) % X], IGX.at[d], ig_send.at[d], ig_recv.at[d], x_peer(d)))
-
 
     piece = dF[pl.ds(pl.multiple_of(y * rows, rows), rows), :]
     for d in range(1, Y):
@@ -334,11 +353,10 @@
     code, tail = pack(piece, scale_for(piece))
     FIN[y, q, : 2 * rows, :] = code
     FIN[y, q, 2 * rows :, :] = tail
+    opposite = Y // 2
+
     def quarter(c):
         return (q + c) % ZL
-
-    def crosses(step, way, c):
-        return step < Y // 2 or c % 2 == way
 
     def ring(step, way, c):
         at = (y - (step - 1)) % Y if way == 0 else (y + (step - 1)) % Y
@@ -352,23 +370,30 @@
 
     def pass_on(step, c):
         for way in range(2):
-            if crosses(step, way, c):
-                ring_arrived(step, way, c)
-                if step < Y // 2 and crosses(step + 1, way, c):
-                    ring(step + 1, way, c)
+            ring_arrived(step, way, c)
+            if step + 1 < opposite:
+                ring(step + 1, way, c)
+
+    def over_z(at, s_sem, r_sem):
+        mine = FIN.at[at, q]
+        for d in range(1, ZL):
+            sends.append(send(mine, mine, s_sem.at[d], r_sem.at[d], zl_peer(d)))
 
     early = list(sends)
     sends.clear()
+    sends.append(send(FIN.at[y, q], FIN.at[y, q], fo_send, fo_recv, y_peer(opposite)))
+    over_z(y, fz_send, fz_recv)
     for way in range(2):
         ring(1, way, 0)
-    for d in range(1, ZL):
-        sends.append(send(FIN.at[y, q], FIN.at[y, q], fz_send.at[d], fz_recv.at[d], zl_peer(d)))
 
     pass_on(1, 0)
     for c in range(1, ZL):
         arrived(FIN.at[y, quarter(c)], fz_recv.at[ZL - c])
         for way in range(2):
             ring(1, way, c)
+    across = (y + opposite) % Y
+    arrived(FIN.at[across, q], fo_recv)
+    over_z(across, fa_send, fa_recv)
 
     @pl.when(r < Y * ZL - 1)
     def _():
@@ -393,38 +418,40 @@
             fg_ref[pl.ds(pl.multiple_of(at * rows, 8), rows), 128 * t : 128 * (t + 1)] = tile
 
     result(y)
-    for step in range(1, Y // 2 + 1):
+    for d in range(1, X):
+        arrived(IXR.at[d], ig_recv.at[d])
+        IGS[...] = IGS[...] + decoded(IXR[d]).reshape(IGS.shape)
+    code, tail = coded(IGS[1 - zh])
+    IZC[:cols, :] = code
+    IZC[cols:, :] = tail
+    sends.append(send(IZC, IZR, ig_send.at[X], ig_recv.at[X], zh_dev))
+    for copy in early:
+        copy.wait_send()
+
+    for step in range(1, opposite):
         for c in range(1, ZL):
             pass_on(step, c)
-        if step < Y // 2:
+        if step + 1 < opposite:
             pass_on(step + 1, 0)
-            result((y - step) % Y)
-            result((y + step) % Y)
-        if step == 1:
-            IGS[...] = IGB[core, x]
-            for d in range(1, X):
-                arrived(IGX.at[d], ig_recv.at[d])
-                IGS[...] = IGS[...] + IGX[d]
-            sends.append(send(IGS.at[1 - zh], IGZ, ig_send.at[X], ig_recv.at[X], zh_dev))
-            for copy in early:
-                copy.wait_send()
-    result((y + Y // 2) % Y)
-
-    OUT = O.at[1]
+        result((y - step) % Y)
+        result((y + step) % Y)
+    for c in range(1, ZL):
+        arrived(FIN.at[across, quarter(c)], fa_recv.at[ZL - c])
+    result(across)
 
     @pl.when(r > 0)
     def _():
         arrived(OR.at[0], o_recv.at[0])
-        OUT[...] = OUT[...] + OR[0]
+        O[...] = O[...] + decoded(OR[0])
 
     @pl.when(r < Y * ZL - 1)
     def _():
         arrived(OR.at[1], o_recv.at[1])
-        OUT[...] = OUT[...] + OR[1]
-
-    out_ref[...] = OUT[...].astype(bf16)
-    arrived(IGZ, ig_recv.at[X])
-    ig_ref[...] = (IGS[zh] + IGZ[...]).astype(bf16)
+        O[...] = O[...] + decoded(OR[1])
+
+    out_ref[...] = O[...].astype(bf16)
+    arrived(IZR, ig_recv.at[X])
+    ig_ref[...] = (IGS[zh] + decoded(IZR[...])).astype(bf16)
 
     for copy in sends:
         copy.wait_send()
@@ -479,13 +506,16 @@
             vmem((Y,) + code, bf16),
             vmem((Y,) + code, bf16),
             vmem((Y, ZL) + code, bf16),
-            vmem((TAPS, chans, width), f32),
-            vmem((2, chans, width), f32),
+            vmem((chans, width), f32),
+            vmem((2, chans + SCALE_ROWS, width), bf16),
+            vmem((2, chans + SCALE_ROWS, width), bf16),
             vmem((CORES, X, ZH, cols, total), f32),
             vmem((X, ZH, cols, total), f32),
-            vmem((X, ZH, cols, total), f32),
+            vmem((X, ZH * cols + SCALE_ROWS, total), bf16),
+            vmem((X, ZH * cols + SCALE_ROWS, total), bf16),
             vmem((ZH, cols, total), f32),
-            vmem((cols, total), f32),
+            vmem((cols + SCALE_ROWS, total), bf16),
+            vmem((cols + SCALE_ROWS, total), bf16),
             dma((3,)),
             dma((15,)), dma((15,)),
             dma((15,)), dma((15,)),
@@ -496,7 +526,9 @@
             dma((2,)), dma((2,)),
             dma((X + 1,)), dma((X + 1,)),
             dma((ZL,)), dma((ZL,)),
-            dma((2, Y, ZL)), dma((2, Y, ZL)),
+            dma((2, Y // 2, ZL)), dma((2, Y // 2, ZL)),
+            dma, dma,
+            dma((ZL,)), dma((ZL,)),
         ],
         compiler_params=pltpu.CompilerParams(
             collective_id=0, has_side_effects=True, vmem_limit_bytes=48 * 1024 * 1024

time: 67.4 us -> 65.5 us (0.972)
  Pallas kernels: 63.9 us -> 62 us
    pallas_call x1, Pallas kernels: 63.9 us -> 62 us  [on_device(): pl.pallas_call(kernel, out_shape=(jax.ShapeDtypeStruct((chans, width), bf...]
where the time goes in v6:
time: 65.5 us; the launch traced here: 65.3 us
  Pallas kernels  62 us (95%)
  local copies, waits for them, and re-layouts  2.67 us (4%)
    pallas_call x1, Pallas kernels, on_device(): pl.pallas_call(kernel, out_shape=(jax.ShapeDtypeStruct((chans, width), bf...  62 us
    unnamed x3, local copies, waits for them, and re-layouts  2.67 us

profile of v6, /device:TPU:1, one launch (start us, length us, event | category | flops | bytes accessed | tf_op | source)
XLA Modules:
  0.0 65.3 jit_solution(14018210105830706809)
XLA Ops:
  0.6 62.0 %shard_map.58 = (bf16[64,512]{1,0:T(8,128)(2,1)S(1)}, bf16[32,1024]{1,0:T(8,128)(2,1)S(1)}, f32[576,1024]{1,0:T(8,128)S(1)}) custom-call(bf16[64,512]{1,0:T(8,128)(2,1)} %bitcast.14, bf16[576,1024]{1,0:T(8,128)(2,1)} %bitcast.13, bf16[64,512]{1,0:T(8,128)(2,1)} %bitcast.15), custom_call_target="tpu_custom_call" | custom-call | tf_op jit(solution)/shard_map/pallas_call | solution.py:490
  62.6 0.6 copy.9
  63.3 0.6 copy.10
  63.9 1.4 %copy.11 = f32[64,9,1024]{2,0,1:T(8,128)} copy(f32[64,9,1024]{2,0,1:T(8,128)S(1)} %bitcast.10) | data formatting | bytes 4718592

commit v7 on v6

--- a/solution.py
+++ b/solution.py
@@ -164,7 +164,7 @@
     others = jnp.where(below, 1, 0) + jnp.where(above, 1, 0)
     pl.semaphore_wait(barrier, len(fixed) + others)
 
-    for d in list(range(ZL, 2 * ZL)) + list(range(1, ZL)):
+    for d in list(range(1, ZL)) + list(range(ZL, 2 * ZL)):
         to = (q + d) % ZL
         sends.append(send(
             G.at[pl.ds(pl.multiple_of(f * chans + to * part, part), part), :], g2_piece(f, q, to),
@@ -173,13 +173,13 @@
 
     def gather_own(block, s_sem, r_sem):
         mine = block(f)
-        for d in range(1, X):
+        for d in (2, 1, 3):
             sends.append(send(mine, mine, s_sem.at[d], r_sem.at[d], x_peer(d)))
         sends.append(send(mine, mine, s_sem.at[4], r_sem.at[4], core_dev))
 
     def gather_other(block, s_sem, r_sem):
         other = block(partner)
-        for d in range(1, X):
+        for d in (2, 1, 3):
             sends.append(send(other, other, s_sem.at[4 + d], r_sem.at[4 + d], x_peer(d)))
         sends.append(send(other, other, s_sem.at[8], r_sem.at[8], core_dev))
 
@@ -290,7 +290,7 @@
         code, tail = pack(dF[rows * k : rows * (k + 1), :], scale)
         codes[k, : 2 * rows, :] = code
         codes[k, 2 * rows :, :] = tail
-    for d in range(1, Y):
+    for d in (4, 3, 5, 2, 6, 1, 7):
         sends.append(send(codes.at[(y + d) % Y], got.at[d], rs_send.at[d], rs_recv.at[d], y_peer(d)))
 
     load_f.wait()
@@ -345,6 +345,14 @@
             device_id=dev(f, r + 1 - a), device_id_type=pl.DeviceIdType.MESH,
         )
 
+    @pl.when(r < Y * ZL - 1)
+    def _():
+        out_copy(0).start()
+
+    @pl.when(r > 0)
+    def _():
+        out_copy(2).start()
+
     piece = dF[pl.ds(pl.multiple_of(y * rows, rows), rows), :]
     for d in range(1, Y):
         arrived(got.at[d], rs_recv.at[d])
@@ -381,10 +389,10 @@
 
     early = list(sends)
     sends.clear()
-    sends.append(send(FIN.at[y, q], FIN.at[y, q], fo_send, fo_recv, y_peer(opposite)))
     over_z(y, fz_send, fz_recv)
     for way in range(2):
         ring(1, way, 0)
+    sends.append(send(FIN.at[y, q], FIN.at[y, q], fo_send, fo_recv, y_peer(opposite)))
 
     pass_on(1, 0)
     for c in range(1, ZL):
@@ -394,14 +402,6 @@
     across = (y + opposite) % Y
     arrived(FIN.at[across, q], fo_recv)
     over_z(across, fa_send, fa_recv)
-
-    @pl.when(r < Y * ZL - 1)
-    def _():
-        out_copy(0).start()
-
-    @pl.when(r > 0)
-    def _():
-        out_copy(2).start()
 
     lane_group = lax.broadcasted_iota(jnp.int32, (rows, 128), 1) // 16
 

time: 65.5 us -> 63 us (0.962)
  the two profiles are of different devices: /device:TPU:1 before, /device:TPU:16 now
where the time goes in v7:
time: 63 us; the launch traced here: 62.8 us
  Pallas kernels  59.5 us (94%)
  local copies, waits for them, and re-layouts  2.67 us (4%)
  between operations  0.64 us (1%)
    pallas_call x1, Pallas kernels, on_device(): pl.pallas_call(kernel, out_shape=(jax.ShapeDtypeStruct((chans, width), bf...  59.5 us
    unnamed x3, local copies, waits for them, and re-layouts  2.67 us

profile of v7, /device:TPU:16, one launch (start us, length us, event | category | flops | bytes accessed | tf_op | source)
XLA Modules:
  0.0 62.8 jit_solution(10222882585452219931)
XLA Ops:
  0.6 59.5 %shard_map.58 = (bf16[64,512]{1,0:T(8,128)(2,1)S(1)}, bf16[32,1024]{1,0:T(8,128)(2,1)S(1)}, f32[576,1024]{1,0:T(8,128)S(1)}) custom-call(bf16[64,512]{1,0:T(8,128)(2,1)} %bitcast.14, bf16[576,1024]{1,0:T(8,128)(2,1)} %bitcast.13, bf16[64,512]{1,0:T(8,128)(2,1)} %bitcast.15), custom_call_target="tpu_custom_call" | custom-call | tf_op jit(solution)/shard_map/pallas_call | solution.py:490
  60.2 0.6 %copy.9 = bf16[1,64,512]{2,1,0:T(8,128)(2,1)} copy(bf16[1,64,512]{2,1,0:T(8,128)(2,1)S(1)} %bitcast.12) | data formatting | bytes 131072
  60.8 0.6 %copy.10 = bf16[1,32,1024]{2,1,0:T(8,128)(2,1)} copy(bf16[1,32,1024]{2,1,0:T(8,128)(2,1)S(1)} %bitcast.11) | data formatting | bytes 131072
  61.4 1.4 %copy.11 = f32[64,9,1024]{2,0,1:T(8,128)} copy(f32[64,9,1024]{2,0,1:T(8,128)S(1)} %bitcast.10) | data formatting | bytes 4718592

commit v8 on v7

--- a/solution.py
+++ b/solution.py
@@ -133,8 +133,8 @@
     def greet(to):
         pl.semaphore_signal(barrier, inc=1, device_id=to, device_id_type=pl.DeviceIdType.MESH)
 
-    fixed = [x_peer(d) for d in range(1, X)] + [zl_peer(d) for d in range(1, ZL)]
-    fixed += [y_peer(d) for d in range(1, Y)] + [core_dev] + [zh_peer(d) for d in range(ZL)]
+    fixed = [zh_peer(d) for d in range(ZL)] + [y_peer(d) for d in (4, 3, 5, 2, 6, 1, 7)]
+    fixed += [zl_peer(d) for d in range(1, ZL)] + [x_peer(d) for d in range(1, X)] + [core_dev]
     for to in fixed:
         greet(to)
 
@@ -206,6 +206,7 @@
         sends.append(send(mine, mine, c_send.at[d], c_recv.at[d], zl_peer(d)))
 
     gather_own(g_block, a_send, a_recv)
+    sends.append(send(g_block(f), g_block(f), a_send.at[0], a_recv.at[0], zh_dev))
 
     def halo_copy(side):
         source, slot, step = (ZL, 0, 1) if side == 0 else (1, ZL + 1, -1)
@@ -233,7 +234,6 @@
     for d in range(1, ZL):
         arrived(g2_piece(f, (q - d) % ZL), p_recv.at[d])
     gather_own(g2_block, b_send, b_recv)
-    sends.append(send(g_block(f), g_block(f), a_send.at[0], a_recv.at[0], zh_dev))
     for d in range(ZL):
         arrived(g2_piece(partner, (q - d) % ZL), p_recv.at[ZL + d])
     gather_other(g2_block, b_send, b_recv)
@@ -428,13 +428,17 @@
     for copy in early:
         copy.wait_send()
 
-    for step in range(1, opposite):
+    def ring_step(step):
         for c in range(1, ZL):
             pass_on(step, c)
         if step + 1 < opposite:
             pass_on(step + 1, 0)
         result((y - step) % Y)
         result((y + step) % Y)
+
+    for step in range(1, opposite - 1):
+        ring_step(step)
+
     for c in range(1, ZL):
         arrived(FIN.at[across, quarter(c)], fa_recv.at[ZL - c])
     result(across)
@@ -452,6 +456,8 @@
     out_ref[...] = O[...].astype(bf16)
     arrived(IZR, ig_recv.at[X])
     ig_ref[...] = (IGS[zh] + decoded(IZR[...])).astype(bf16)
+
+    ring_step(opposite - 1)
 
     for copy in sends:
         copy.wait_send()

time: 63 us -> 62.2 us (0.987)
  Pallas kernels: 59.5 us -> 58.8 us
    pallas_call x1, Pallas kernels: 59.5 us -> 58.8 us  [on_device(): pl.pallas_call(kernel, out_shape=(jax.ShapeDtypeStruct((chans, width), bf...]
where the time goes in v8:
time: 62.2 us; the launch traced here: 62.1 us
  Pallas kernels  58.8 us (95%)
  local copies, waits for them, and re-layouts  2.67 us (4%)
  between operations  0.64 us (1%)
    pallas_call x1, Pallas kernels, on_device(): pl.pallas_call(kernel, out_shape=(jax.ShapeDtypeStruct((chans, width), bf...  58.8 us
    unnamed x3, local copies, waits for them, and re-layouts  2.67 us

profile of v8, /device:TPU:16, one launch (start us, length us, event | category | flops | bytes accessed | tf_op | source)
XLA Modules:
  0.0 62.1 jit_solution(9335160704371191148)
XLA Ops:
  0.6 58.8 %shard_map.58 = (bf16[64,512]{1,0:T(8,128)(2,1)S(1)}, bf16[32,1024]{1,0:T(8,128)(2,1)S(1)}, f32[576,1024]{1,0:T(8,128)S(1)}) custom-call(bf16[64,512]{1,0:T(8,128)(2,1)} %bitcast.14, bf16[576,1024]{1,0:T(8,128)(2,1)} %bitcast.13, bf16[64,512]{1,0:T(8,128)(2,1)} %bitcast.15), custom_call_target="tpu_custom_call" | custom-call | tf_op jit(solution)/shard_map/pallas_call | solution.py:496
  59.4 0.6 %copy.9 = bf16[1,64,512]{2,1,0:T(8,128)(2,1)} copy(bf16[1,64,512]{2,1,0:T(8,128)(2,1)S(1)} %bitcast.12) | data formatting | bytes 131072
  60.0 0.6 %copy.10 = bf16[1,32,1024]{2,1,0:T(8,128)(2,1)} copy(bf16[1,32,1024]{2,1,0:T(8,128)(2,1)S(1)} %bitcast.11) | data formatting | bytes 131072
  60.7 1.4 %copy.11 = f32[64,9,1024]{2,0,1:T(8,128)} copy(f32[64,9,1024]{2,0,1:T(8,128)S(1)} %bitcast.10) | data formatting | bytes 4718592

commit v9 on v8

--- a/solution.py
+++ b/solution.py
@@ -96,6 +96,10 @@
     def y_peer(d):
         return dev(f, ((y + d) % Y) * ZL + q)
 
+    z_first = ZL - 1 - (q + 1) // 2
+    z_second = jnp.where((q == 0) | (q == ZL - 1), 2, 1)
+    z_order = z_first, z_second, 6 - z_first - z_second
+
     partner = f + CORES - 2 * CORES * zh
     sibling = f + 1 - 2 * core
     zh_dev, core_dev = dev(partner, r), dev(sibling, r)
@@ -201,7 +205,7 @@
                 k = x_from + CORES * (zh if second == 0 else 1 - zh)
                 arrived(block(k), r_sem.at[9 + 2 * (d - 1) + second])
 
-    for d in range(1, ZL):
+    for d in z_order:
         mine = cots.at[q + 1]
         sends.append(send(mine, mine, c_send.at[d], c_recv.at[d], zl_peer(d)))
 
@@ -286,12 +290,12 @@
     dF[2 * stack :, :] += grad_term(2, 0, 1)
     rows = TAPS * stack // Y
     scale = scale_for(dF[...])
-    for k in range(Y):
-        code, tail = pack(dF[rows * k : rows * (k + 1), :], scale)
-        codes[k, : 2 * rows, :] = code
-        codes[k, 2 * rows :, :] = tail
     for d in (4, 3, 5, 2, 6, 1, 7):
-        sends.append(send(codes.at[(y + d) % Y], got.at[d], rs_send.at[d], rs_recv.at[d], y_peer(d)))
+        at = pl.multiple_of(((y + d) % Y) * rows, rows)
+        code, tail = pack(dF[pl.ds(at, rows), :], scale)
+        codes[d, : 2 * rows, :] = code
+        codes[d, 2 * rows :, :] = tail
+        sends.append(send(codes.at[d], got.at[d], rs_send.at[d], rs_recv.at[d], y_peer(d)))
 
     load_f.wait()
     groups = X * ZH * CORES
@@ -384,7 +388,7 @@
 
     def over_z(at, s_sem, r_sem):
         mine = FIN.at[at, q]
-        for d in range(1, ZL):
+        for d in z_order:
             sends.append(send(mine, mine, s_sem.at[d], r_sem.at[d], zl_peer(d)))
 
     early = list(sends)

time: 62.2 us -> 62 us (level)
  the two profiles are of different devices: /device:TPU:16 before, /device:TPU:1 now
where the time goes in v9:
time: 62 us; the launch traced here: 61.7 us
  Pallas kernels  58.4 us (94%)
  local copies, waits for them, and re-layouts  2.67 us (4%)
  between operations  0.64 us (1%)
    pallas_call x1, Pallas kernels, on_device(): pl.pallas_call(kernel, out_shape=(jax.ShapeDtypeStruct((chans, width), bf...  58.4 us
    unnamed x3, local copies, waits for them, and re-layouts  2.67 us

profile of v9, /device:TPU:1, one launch (start us, length us, event | category | flops | bytes accessed | tf_op | source)
XLA Modules:
  0.0 61.7 jit_solution(16300567143188982965)
XLA Ops:
  0.6 58.4 %shard_map.58 = (bf16[64,512]{1,0:T(8,128)(2,1)S(1)}, bf16[32,1024]{1,0:T(8,128)(2,1)S(1)}, f32[576,1024]{1,0:T(8,128)S(1)}) custom-call(bf16[64,512]{1,0:T(8,128)(2,1)} %bitcast.14, bf16[576,1024]{1,0:T(8,128)(2,1)} %bitcast.13, bf16[64,512]{1,0:T(8,128)(2,1)} %bitcast.15), custom_call_target="tpu_custom_call" | custom-call | tf_op jit(solution)/shard_map/pallas_call | solution.py:500
  59.1 0.6 %copy.9 = bf16[1,64,512]{2,1,0:T(8,128)(2,1)} copy(bf16[1,64,512]{2,1,0:T(8,128)(2,1)S(1)} %bitcast.12) | data formatting | bytes 131072
  59.7 0.6 %copy.10 = bf16[1,32,1024]{2,1,0:T(8,128)(2,1)} copy(bf16[1,32,1024]{2,1,0:T(8,128)(2,1)S(1)} %bitcast.11) | data formatting | bytes 131072
  60.3 1.4 %copy.11 = f32[64,9,1024]{2,0,1:T(8,128)} copy(f32[64,9,1024]{2,0,1:T(8,128)S(1)} %bitcast.10) | data formatting | bytes 4718592
